TPU v7x, 32 devices: a whole 2x2x4 slice. The times are simulated.
32 devices in a mesh: dp: 2 (over core), expert: 4 (over y, x), tensor: 4 (over z).
Axes of the slice: x: 2, y: 2, z: 4, core: 2. Of those that a mesh axis runs over, the one named last changes fastest.
Arguments:
- out_grad: bfloat16 [2, 512, 6144], P('dp', ('expert', 'tensor')), may hold values from -4 to 4
- routes: int32 [2, 512, 2], P('dp', ('expert', 'tensor')), may hold values from 0 to 3, all different within a row; in each aligned block of 32 rows (0 to 31, 32 to 63, ..., all dimensions but the last counted through in order) at most 32 rows name the same one
- route_weight: bfloat16 [2, 512, 2], P('dp', ('expert', 'tensor')), may hold values from 0.19921875 to 0.796875
- gate_pre: bfloat16 [2, 4, 512, 8192], P('dp', 'expert', None, 'tensor'), may hold values from -8 to 8
- up_pre: bfloat16 [2, 4, 512, 8192], P('dp', 'expert', None, 'tensor'), may hold values from -6 to 6
- down_weight: bfloat16 [4, 8192, 6144], P('expert', 'tensor', 'dp'), may hold values from -0.0625 to 0.0625
Outputs:
- route_grad: float32 [2, 512, 2], P('dp', ('expert', 'tensor'))
- gate_grad: bfloat16 [2, 4, 512, 8192], P('dp', 'expert', None, 'tensor')
- up_grad: bfloat16 [2, 4, 512, 8192], P('dp', 'expert', None, 'tensor')
- down_grad: bfloat16 [4, 8192, 6144], P('expert', 'tensor', 'dp')
Inputs may be any that keep to these rules, and one draw needn't show every extreme that they name: `routes`: the two experts of a token differ. Among the tokens of one shard (32 tokens in a row, aligned) no expert is named more than 32 times, and in every draw some expert is named exactly 32 times by the tokens of some shard.
All inputs are finite; a program needn't handle non-finite values.
Results may differ from a plain program's by a relative error of at most 0.008.
Values may be sent and summed in bfloat16 or wider, within the bound.
A program may use at most 128 MiB of HBM per device.

v0:
```python
import jax
import jax.numpy as jnp
from jax import lax
from jax.sharding import PartitionSpec as P


def silu_parts(gate):
    sig = jax.nn.sigmoid(gate)
    return (gate * sig, sig * (1.0 + gate * (1.0 - sig)))


def shards(out_grad, routes, route_weight, gate_pre, up_pre, down_weight):
    experts = lax.axis_size("expert")
    tensor_size = lax.axis_size("tensor")
    rows = gate_pre.shape[2]
    capacity = rows // (experts * tensor_size)
    tok_rows = out_grad.shape[1]
    width = out_grad.shape[2]
    flat_routes = routes[0].reshape(2 * tok_rows)
    onehot = (flat_routes[:, None] == jnp.arange(experts, dtype=jnp.int32)[None, :]).astype(
        jnp.int32
    )
    position = jnp.cumsum(onehot, axis=0) - 1
    slot = jnp.sum(onehot * position, axis=1)
    target = flat_routes * capacity + slot
    placing = jnp.arange(experts * capacity, dtype=jnp.int32)[:, None] == target[None, :]
    place_tok = jnp.any(placing.reshape(experts * capacity, tok_rows, 2), axis=2)
    send_grad = jnp.dot(
        place_tok.astype(jnp.bfloat16), out_grad[0], preferred_element_type=jnp.float32
    ).astype(jnp.bfloat16)
    flat_weight = route_weight[0].reshape(2 * tok_rows).astype(jnp.float32)
    send_weight = jnp.sum(jnp.where(placing, flat_weight[None, :], 0.0), axis=1).astype(
        jnp.bfloat16
    )
    grad_copies = jnp.broadcast_to(
        send_grad.reshape(experts, 1, capacity, width), (experts, tensor_size, capacity, width)
    ).reshape(experts * tensor_size, capacity, width)
    weight_copies = jnp.broadcast_to(
        send_weight.reshape(experts, 1, capacity), (experts, tensor_size, capacity)
    ).reshape(experts * tensor_size, capacity)
    routed_grad, routed_weight = (
        lax.all_to_all(grad_copies, ("expert", "tensor"), split_axis=0, concat_axis=0, tiled=True),
        lax.all_to_all(
            weight_copies, ("expert", "tensor"), split_axis=0, concat_axis=0, tiled=True
        ),
    )
    routed_grad = routed_grad.reshape(rows, width)
    scale = routed_weight.reshape(rows).astype(jnp.float32)[:, None]
    weight_full = lax.all_gather(down_weight, "dp", axis=2, tiled=True)[0]
    gate = gate_pre[0, 0].astype(jnp.float32)
    upper = up_pre[0, 0].astype(jnp.float32)
    act, slope = silu_parts(gate)
    hidden = (act * upper).astype(jnp.bfloat16)
    back = lax.dot_general(
        routed_grad, weight_full, (((1,), (1,)), ((), ())), preferred_element_type=jnp.float32
    )
    hidden_grad = scale * back
    gate_grad = (hidden_grad * upper * slope).astype(jnp.bfloat16)
    up_grad = (hidden_grad * act).astype(jnp.bfloat16)
    scaled = (scale * routed_grad).astype(jnp.bfloat16)
    part = lax.dot_general(
        hidden, scaled, (((0,), (0,)), ((), ())), preferred_element_type=jnp.float32
    )
    down_grad = lax.psum_scatter(
        part[None].astype(jnp.bfloat16), "dp", scatter_dimension=2, tiled=True
    )
    score = jnp.sum(hidden.astype(jnp.float32) * back, axis=1)
    total = lax.psum(score, "tensor")
    mine = lax.dynamic_index_in_dim(
        total.reshape(experts, tensor_size, capacity), lax.axis_index("tensor"), 1, keepdims=False
    )
    returned = lax.all_to_all(mine, "expert", split_axis=0, concat_axis=0, tiled=True)
    flat_back = returned.reshape(experts * capacity)
    route_grad = jnp.sum(jnp.where(placing, flat_back[:, None], 0.0), axis=0).reshape(
        1, tok_rows, 2
    )
    return (route_grad, gate_grad[None, None], up_grad[None, None], down_grad)


def solution(mesh):
    in_specs = (
        P("dp", ("expert", "tensor"), None),
        P("dp", ("expert", "tensor"), None),
        P("dp", ("expert", "tensor"), None),
        P("dp", "expert", None, "tensor"),
        P("dp", "expert", None, "tensor"),
        P("expert", "tensor", "dp"),
    )
    out_specs = (
        P("dp", ("expert", "tensor"), None),
        P("dp", "expert", None, "tensor"),
        P("dp", "expert", None, "tensor"),
        P("expert", "tensor", "dp"),
    )
    return jax.shard_map(shards, mesh=mesh, in_specs=in_specs, out_specs=out_specs, check_vma=False)
```

profile of v0, /device:TPU:0, one launch (start us, length us, event | category | flops | bytes accessed | tf_op | source)
XLA Modules:
  0.0 283.7 jit_solution(12942093631047495112)
XLA Ops:
  7.2 0.7 all-gather.2.cloned.1.call-update
  8.0 0.1 reshape_squeeze.4
  8.2 0.1 reduce_window_sum.11
  8.3 0.2 select_reduce_fusion.2
  8.5 0.1 reduce_sum.39
  8.8 0.6 convolution_convert_fusion
  9.4 3.6 %broadcast_in_dim.49 = bf16[4,4,32,6144]{3,2,1,0:T(8,128)(2,1)} broadcast(bf16[4,32,6144]{2,1,0:T(8,128)(2,1)S(1)} %bitcast.76), dimensions={0,2,3} | broadcast | bytes 7864320 | tf_op jit(solution)/shard_map/broadcast_in_dim | solution.py:35
  13.0 8.5 %all-to-all-start = ((bf16[16,32,6144]{2,1,0:T(8,128)(2,1)}), bf16[16,32,6144]{2,1,0:T(8,128)(2,1)}, u32[]{:S(2)}, u32[]{:S(2)}) async-start(bf16[16,32,6144]{2,1,0:T(8,128)(2,1)} %bitcast.74), calls=%async_computation | async-start | bytes 12582912 | tf_op jit(solution)/shard_map/all_to_all | solution.py:42
  21.5 149.0 %all-to-all-done = bf16[16,32,6144]{2,1,0:T(8,128)(2,1)} async-done(((bf16[16,32,6144]{2,1,0:T(8,128)(2,1)}), bf16[16,32,6144]{2,1,0:T(8,128)(2,1)}, u32[]{:S(2)}, u32[]{:S(2)}) %all-to-all-start) | async-done | bytes 6291488 | tf_op jit(solution)/shard_map/all_to_all | solution.py:42
  170.5 20.4 %multiply_reduce_fusion = (f32[512]{0:T(512)S(1)}, f32[512,2048]{1,0:T(8,128)}) fusion(bf16[1,1,512,2048]{3,2,1,0:T(8,128)(2,1)S(1)} %copy-done.2, bf16[1,1,512,2048]{3,2,1,0:T(8,128)(2,1)} %param.9, bf16[512,6144]{1,0:T(8,128)(2,1)} %bitcast.6, bf16[1,2048,6144]{2,1,0:T(8,128)(2,1)} %all-gather.2.cloned.1.call-done), kind=kOutput, calls=%fused_computation.28 | convolution fusion | flops 12896436224 | bytes 39847936 | tf_op jit(solution)/shard_map/dot_general | solution.py:54
  190.9 8.5 %psum.7 = f32[4,4,32]{2,1,0:T(4,128)S(1)} all-reduce(f32[4,4,32]{2,1,0:T(4,128)S(1)} %reshape.93), channel_id=1, replica_groups=mesh['dp'=2,'expert'=4,'tensor'=4] {'tensor'}, use_global_device_ids=true, to_apply=%region_4.5 | all-reduce | flops 512 | bytes 4096 | tf_op jit(solution)/shard_map/psum | solution.py:68
  199.4 0.6 constant_dynamic-slice_fusion
  200.0 3.2 %all-to-all-start.1 = ((f32[4,1,32]{2,1,0:T(1,128)}), f32[4,1,32]{2,1,0:T(1,128)S(1)}, u32[]{:S(2)}, u32[]{:S(2)}) async-start(f32[4,1,32]{2,1,0:T(1,128)} %constant_dynamic-slice_fusion), calls=%async_computation.1 | async-start | bytes 4096 | tf_op jit(solution)/shard_map/all_to_all | solution.py:72
  203.4 0.1 reshape.97
  203.5 4.3 %all-to-all-done.1 = f32[4,1,32]{2,1,0:T(1,128)S(1)} async-done(((f32[4,1,32]{2,1,0:T(1,128)}), f32[4,1,32]{2,1,0:T(1,128)S(1)}, u32[]{:S(2)}, u32[]{:S(2)}) %all-to-all-start.1) | async-done | bytes 544 | tf_op jit(solution)/shard_map/all_to_all | solution.py:72
  207.8 0.5 broadcast.51
  208.3 0.7 reduce.7
  209.1 0.2 select_reduce_fusion
  209.3 10.5 %all_to_all.20 = bf16[16,1,32]{2,1,0:T(2,128)(2,1)S(1)} all-to-all(bf16[16,1,32]{2,1,0:T(2,128)(2,1)S(1)} %copy.34), channel_id=1, replica_groups=mesh['dp'=2,'expert'=4,'tensor'=4] {'expert','tensor'}, dimensions={0} | all-to-all | bytes 2048 | tf_op jit(solution)/shard_map/all_to_all | solution.py:43
  219.8 4.8 %multiply_convert_fusion = bf16[16,32,6144]{2,1,0:T(8,128)(2,1)S(1)} fusion(bf16[16,32,6144]{2,1,0:T(8,128)(2,1)} %all-to-all-done, f32[16,32]{1,0:T(8,128)S(1)} %bitcast.77), kind=kLoop, calls=%fused_computation.3 | loop fusion | flops 9437184 | bytes 12584960 | tf_op jit(solution)/shard_map/convert_element_type | solution.py:60
  224.6 20.2 %convert_bitcast_fusion = bf16[1,2048,6144]{2,1,0:T(8,128)(2,1)} fusion(bf16[512,6144]{1,0:T(8,128)(2,1)S(1)} %bitcast.75, bf16[1,1,512,2048]{3,2,1,0:T(8,128)(2,1)S(1)} %copy-done.2, bf16[1,1,512,2048]{3,2,1,0:T(8,128)(2,1)} %param.9), kind=kOutput, calls=%fused_computation.2 | convolution fusion | flops 12905873408 | bytes 35651584 | tf_op jit(solution)/shard_map/dot_general | solution.py:61
  245.0 0.6 copy.35
  245.7 6.4 %fusion.19 = (bf16[1,1,512,2048]{3,2,1,0:T(8,128)(2,1)}, bf16[1,1,512,2048]{3,2,1,0:T(8,128)(2,1)}) fusion(f32[512,2048]{1,0:T(8,128)} %get-tuple-element.29, f32[512]{0:T(512)S(1)} %reshape.98, bf16[1,1,512,2048]{3,2,1,0:T(8,128)(2,1)} %param.9, bf16[1,1,512,2048]{3,2,1,0:T(8,128)(2,1)S(1)} %copy-done.2), kind=kLoop, calls=%fused_computation.29 | loop fusion | flops 16777216 | bytes 12584960 | tf_op jit(solution)/shard_map/broadcast_in_dim | solution.py:77
  252.1 24.7 %reduce-scatter.2.cloned.1.call-done = bf16[1,2048,3072]{2,1,0:T(8,128)(2,1)} async-done(((bf16[1,2048,6144]{2,1,0:T(8,128)(2,1)}), bf16[1,2048,3072]{2,1,0:T(8,128)(2,1)}) %reduce-scatter.2.cloned.1.call-update) | async-done | bytes 12582928 | tf_op jit(solution)/shard_map/reduce_scatter | solution.py:64
  (30 shorter events, 1.0 us)
Async XLA Ops:
  7.2 1.6 copy-start
  7.2 0.7 copy-start.3
  7.2 163.3 %all-gather.2.cloned.1.call-start = ((), (), s32[]{:S(2)}) async-start(), calls=%async_computation.4 | async-start | bytes 37748736 | tf_op jit(solution)/shard_map/all_gather | solution.py:49
  13.0 157.5 %copy-start.2 = (bf16[1,1,512,2048]{3,2,1,0:T(8,128)(2,1)S(1)}, bf16[1,1,512,2048]{3,2,1,0:T(8,128)(2,1)}, u32[]{:S(2)}) copy-start(bf16[1,1,512,2048]{3,2,1,0:T(8,128)(2,1)} %param.10) | copy-start | bytes 6291460
  13.0 157.5 %all-to-all-start = ((bf16[16,32,6144]{2,1,0:T(8,128)(2,1)}), bf16[16,32,6144]{2,1,0:T(8,128)(2,1)}, u32[]{:S(2)}, u32[]{:S(2)}) async-start(bf16[16,32,6144]{2,1,0:T(8,128)(2,1)} %bitcast.74), calls=%async_computation | async-start | bytes 12582912 | tf_op jit(solution)/shard_map/all_to_all | solution.py:42
  170.5 32.8 %copy-start.4 = (bf16[1,32,2]{1,2,0:T(2,128)(2,1)S(1)}, bf16[1,32,2]{1,2,0:T(2,128)(2,1)}, u32[]{:S(2)}) copy-start(bf16[1,32,2]{1,2,0:T(2,128)(2,1)} %param.8) | copy-start | bytes 388
  200.0 7.8 %all-to-all-start.1 = ((f32[4,1,32]{2,1,0:T(1,128)}), f32[4,1,32]{2,1,0:T(1,128)S(1)}, u32[]{:S(2)}, u32[]{:S(2)}) async-start(f32[4,1,32]{2,1,0:T(1,128)} %constant_dynamic-slice_fusion), calls=%async_computation.1 | async-start | bytes 4096 | tf_op jit(solution)/shard_map/all_to_all | solution.py:72
  203.3 73.6 %reduce-scatter.2.cloned.1.call-start = ((), (), s32[]{:S(2)}) async-start(), calls=%async_computation.5 | async-start | bytes 37748736 | tf_op jit(solution)/shard_map/reduce_scatter | solution.py:64
  245.7 31.1 %copy-start.1 = (bf16[1,32,6144]{2,1,0:T(8,128)(2,1)S(1)}, bf16[1,32,6144]{2,1,0:T(8,128)(2,1)}, u32[]{:S(2)}) copy-start(bf16[1,32,6144]{2,1,0:T(8,128)(2,1)} %param.6) | copy-start | bytes 1179652
Sparse Core Ops, SparseCore 0:
  9.6 45.2 all-gather.1
  245.0 31.8 reduce-scatter.1
where the time goes:
time: 284 us
  waiting for transfers between devices  179 us (63%)
  matrix products  41.2 us (15%)
  blocking collectives  19 us (7%)
  between operations  14.2 us (5%)
  other arithmetic  12.5 us (4%)
  starting transfers between devices  11.8 us (4%)
  local copies, waits for them, and re-layouts  6.39 us (2%)
    all_to_all x1, waiting for transfers between devices, shards(): lax.all_to_all(grad_copies, ('expert', 'tensor'), split_axis=0, concat_ax...  149 us
    reduce_scatter x1, waiting for transfers between devices, shards(): lax.psum_scatter(part[None].astype(jnp.bfloat16), 'dp', scatter_dimension...  24.7 us
    dot_general x1, matrix products, shards(): lax.dot_general(routed_grad, weight_full, (((1,), (1,)), ((), ())), prefe...  20.4 us
    dot_general x1, matrix products, shards(): lax.dot_general(hidden, scaled, (((0,), (0,)), ((), ())), preferred_eleme...  20.2 us
    all_to_all x1, blocking collectives, shards(): lax.all_to_all(weight_copies, ('expert', 'tensor'), split_axis=0, concat_...  10.5 us
    all_to_all x1, starting transfers between devices, shards(): lax.all_to_all(grad_copies, ('expert', 'tensor'), split_axis=0, concat_ax...  8.49 us
    psum x1, blocking collectives, shards(): total = lax.psum(score, 'tensor')  8.49 us
    broadcast_in_dim x1, other arithmetic, shards(): return (route_grad, gate_grad[None, None], up_grad[None, None], down_grad)  6.41 us
  transfers between devices with their start and end apart: 4, of which 3 were waited for; matrix products, arithmetic and copies ran while one was open for 4% of the time, Pallas kernels for 0%

commit v1 on v0

v1 whole, which is shorter than its diff:
```python
import jax
import jax.numpy as jnp
from jax import lax
from jax.sharding import PartitionSpec as P

BF = jnp.bfloat16
F32 = jnp.float32


def swap(x):
    return lax.ppermute(x, "dp", [(0, 1), (1, 0)])


def shards(out_grad, routes, route_weight, gate_pre, up_pre, down_weight):
    me = lax.axis_index("dp")
    expert = lax.axis_index("expert")
    n = lax.axis_size("expert") * lax.axis_size("tensor")
    rows = gate_pre.shape[2]
    cap = rows // n
    tok, width = out_grad.shape[1:]
    half = width // 2
    first = me == 0

    def ordered(mine, other):
        return jnp.where(first, mine, other), jnp.where(first, other, mine)

    meta = jnp.concatenate([routes[0].T.astype(F32), route_weight[0].T.astype(F32)], axis=0)
    meta = lax.all_gather(meta, ("dp", "expert", "tensor"), axis=0)
    meta = meta.reshape(2, n, 4, tok)

    low, high = out_grad[0, :, :half], out_grad[0, :, half:]
    keep = jnp.where(first, low, high)
    other = swap(jnp.where(first, high, low))
    both = jnp.stack(ordered(keep, other))
    tokens = lax.all_gather(both, ("expert", "tensor"), axis=1)

    hits = meta[:, :, :2] == expert.astype(F32)
    taken = jnp.any(hits, axis=2)
    before = jnp.arange(tok)[:, None] > jnp.arange(tok)[None, :]
    slot = jnp.sum(jnp.where(taken[:, :, None, :] & before, 1, 0), axis=3)
    place = taken[:, :, None, :] & (slot[:, :, None, :] == jnp.arange(cap)[:, None])
    tok_weight = jnp.sum(jnp.where(hits, meta[:, :, 2:], 0.0), axis=2)
    scale = jnp.sum(jnp.where(place, tok_weight[:, :, None, :], 0.0), axis=3)
    scale = scale.reshape(2 * rows, 1)

    group = max(1, min(n, 256 // tok))
    eye = jnp.eye(group, dtype=bool)
    wide = place.reshape(2, n // group, group, cap, 1, tok) & eye[:, None, :, None]
    wide = wide.reshape(2 * n // group, group * cap, group * tok).astype(BF)
    routed = lax.dot_general(
        wide,
        tokens.reshape(2 * n // group, group * tok, half),
        (((2,), (1,)), ((0,), (0,))),
        preferred_element_type=F32,
    ).reshape(2 * rows, half)
    routed = routed.astype(BF)

    gate = gate_pre[0, 0].astype(F32)
    upper = up_pre[0, 0].astype(F32)
    sig = jax.nn.sigmoid(gate)
    act = gate * sig
    slope = sig * (1.0 + gate * (1.0 - sig))
    hidden = (act * upper).astype(BF)
    hidden_both = jnp.concatenate(ordered(hidden, swap(hidden)), axis=0)

    back = lax.dot_general(
        routed, down_weight[0], (((1,), (1,)), ((), ())), preferred_element_type=F32
    ).reshape(2, rows, -1)
    sent = lax.dynamic_index_in_dim(back, 1 - me, 0, keepdims=False).astype(BF)
    back = lax.dynamic_index_in_dim(back, me, 0, keepdims=False) + swap(sent).astype(F32)

    scaled = (scale * routed).astype(BF)
    down_grad = lax.dot_general(
        hidden_both, scaled, (((0,), (0,)), ((), ())), preferred_element_type=F32
    ).astype(BF)

    my_scale = lax.dynamic_slice_in_dim(scale, me * rows, rows, 0)
    hidden_grad = my_scale * back
    gate_grad = (hidden_grad * upper * slope).astype(BF)
    up_grad = (hidden_grad * act).astype(BF)
    score = jnp.sum(hidden.astype(F32) * back, axis=1).reshape(n, cap, 1)
    my_place = lax.dynamic_index_in_dim(place, me, 0, keepdims=False)
    my_hits = lax.dynamic_index_in_dim(hits, me, 0, keepdims=False)
    tok_score = jnp.sum(jnp.where(my_place, score, 0.0), axis=1)
    pair = jnp.where(my_hits, tok_score[:, None, :], 0.0)
    pair = lax.psum_scatter(pair, ("expert", "tensor"), scatter_dimension=0, tiled=True)
    route_grad = pair.reshape(2, tok).T[None]
    return (route_grad, gate_grad[None, None], up_grad[None, None], down_grad[None])


def solution(mesh):
    in_specs = (
        P("dp", ("expert", "tensor"), None),
        P("dp", ("expert", "tensor"), None),
        P("dp", ("expert", "tensor"), None),
        P("dp", "expert", None, "tensor"),
        P("dp", "expert", None, "tensor"),
        P("expert", "tensor", "dp"),
    )
    out_specs = (
        P("dp", ("expert", "tensor"), None),
        P("dp", "expert", None, "tensor"),
        P("dp", "expert", None, "tensor"),
        P("expert", "tensor", "dp"),
    )
    return jax.shard_map(shards, mesh=mesh, in_specs=in_specs, out_specs=out_specs, check_vma=False)
```

time: 284 us -> 254 us (0.89)
  waiting for transfers between devices: 179 us -> 25.9 us
  blocking collectives: 19 us -> 146 us
  starting transfers between devices: 11.8 us -> 0.7 us
  other arithmetic: 12.5 us -> 17.4 us
    all_to_all x2 -> x0, waiting for transfers between devices: 153 us -> none  [the longest x1 149 us: shards(): lax.all_to_all(grad_copies, ('expert', 'tensor'), split_axis=0, concat_ax...]
    unnamed x0 -> x1, blocking collectives: none -> 74.5 us
    all_gather x0 -> x1, blocking collectives: none -> 71.7 us  [shards(): meta = lax.all_gather(meta, ('dp', 'expert', 'tensor'), axis=0)]
    reduce_scatter x1 -> x0, waiting for transfers between devices: 24.7 us -> none  [shards(): lax.psum_scatter(part[None].astype(jnp.bfloat16), 'dp', scatter_dimension...]
    all_gather x1, waiting for transfers between devices: 0.01 us -> 20.8 us  [shards(): tokens = lax.all_gather(both, ('expert', 'tensor'), axis=1)]
    all_to_all x2 -> x0, starting transfers between devices: 11.7 us -> none  [the longest x1 8.49 us: shards(): lax.all_to_all(grad_copies, ('expert', 'tensor'), split_axis=0, concat_ax...]
    all_to_all x1 -> x0, blocking collectives: 10.5 us -> none  [shards(): lax.all_to_all(weight_copies, ('expert', 'tensor'), split_axis=0, concat_...]
    psum x1 -> x0, blocking collectives: 8.49 us -> none  [shards(): total = lax.psum(score, 'tensor')]
  transfers between devices with their start and end apart: 4 -> 4, of which waited for: 3 -> 3; matrix products, arithmetic and copies ran while one was open for 4% -> 3% of each run, Pallas kernels for 0% -> 0%
where the time goes in v1:
time: 254 us
  blocking collectives  146 us (57%)
  matrix products  41.3 us (16%)
  waiting for transfers between devices  25.9 us (10%)
  other arithmetic  17.4 us (7%)
  between operations  14.2 us (6%)
  local copies, waits for them, and re-layouts  8.44 us (3%)
    unnamed x1, blocking collectives  74.5 us
    all_gather x1, blocking collectives, shards(): meta = lax.all_gather(meta, ('dp', 'expert', 'tensor'), axis=0)  71.7 us
    all_gather x1, waiting for transfers between devices, shards(): tokens = lax.all_gather(both, ('expert', 'tensor'), axis=1)  20.8 us
    dot_general x1, matrix products, shards(): lax.dot_general(hidden_both, scaled, (((0,), (0,)), ((), ())), preferred_...  18.7 us
    dot_general x1, matrix products, shards(): lax.dot_general(routed, down_weight[0], (((1,), (1,)), ((), ())), preferr...  18 us
    reduce_sum x1, other arithmetic, shards(): score = jnp.sum(hidden.astype(F32) * back, axis=1).reshape(n, cap, 1)  7.68 us
  transfers between devices with their start and end apart: 4, of which 3 were waited for; matrix products, arithmetic and copies ran while one was open for 3% of the time, Pallas kernels for 0%

profile of v1, /device:TPU:0, one launch (start us, length us, event | category | flops | bytes accessed | tf_op | source)
XLA Modules:
  0.0 254.0 jit_solution(12066234450863929870)
XLA Ops:
  7.2 1.0 select_bitcast_fusion
  8.3 0.5 collective-permute-start
  8.8 1.1 collective-permute-done
  9.9 1.1 fusion.23
  10.9 0.8 pad_maximum_fusion
  11.9 0.4 and.61
  12.3 0.7 convert_bitcast_fusion.1
  13.0 0.7 convert_bitcast_fusion.2
  13.6 71.7 %all-gather.2 = f32[32,4,32]{2,1,0:T(4,128)S(1)} all-gather(f32[1,4,32]{2,1,0:T(4,128)S(1)} %maximum_bitcast_fusion), channel_id=2, replica_groups=mesh['dp'=2,'expert'=4,'tensor'=4] {'dp','expert','tensor'}, dimensions={0}, use_global_device_ids=true | all-gather | bytes 16896 | tf_op jit(solution)/shard_map/all_gather | solution.py:28
  85.5 0.6 select_reduce_fusion.1
  86.2 0.6 and.58
  86.8 1.5 and.59
  88.4 20.8 %all-gather.5.cloned.1.call-done = bf16[2,512,3072]{2,1,0:T(8,128)(2,1)} async-done(((bf16[2,32,3072]{2,1,0:T(8,128)(2,1)}), bf16[2,512,3072]{2,1,0:T(8,128)(2,1)}) %all-gather.5.cloned.1.call-update) | async-done | bytes 6291472 | tf_op jit(solution)/shard_map/all_gather | solution.py:35
  109.2 4.6 %convolution_convert_fusion = bf16[4,256,3072]{2,1,0:T(8,128)(2,1)S(1)} fusion(bf16[4,256,3072]{2,1,0:T(8,128)(2,1)} %bitcast.89, pred[4,256,256]{2,1,0:T(32,128)(4,1)S(1)} %and.59, pred[256,256]{1,0:T(8,128)(4,1)S(1)} %and.61), kind=kOutput, calls=%fused_computation.9 | convolution fusion | flops 1614020608 | bytes 12910592 | tf_op jit(solution)/shard_map/dot_general | solution.py:50
  113.8 18.0 %fusion.1 = f32[2,512,2048]{2,1,0:T(8,128)S(1)} fusion(bf16[2,512,3072]{2,1,0:T(8,128)(2,1)S(1)} %bitcast.87, bf16[1,2048,3072]{2,1,0:T(8,128)(2,1)} %param.11), kind=kOutput, calls=%fused_computation.2 | convolution fusion | flops 12884901888 | bytes 27262976 | tf_op jit(solution)/shard_map/dot_general | solution.py:66
  132.1 3.1 %copy-done.2 = f32[2,512,2048]{2,1,0:T(8,128)} copy-done((f32[2,512,2048]{2,1,0:T(8,128)}, f32[2,512,2048]{2,1,0:T(8,128)S(1)}, u32[]{:S(2)}) %copy-start.2) | copy-done | bytes 8388632
  135.5 4.0 %collective-permute-done.1 = bf16[512,2048]{1,0:T(8,128)(2,1)} collective-permute-done((bf16[512,2048]{1,0:T(8,128)(2,1)S(1)}, bf16[512,2048]{1,0:T(8,128)(2,1)}, u32[]{:S(2)}, u32[]{:S(2)}) %collective-permute-start.1) | collective-permute-done | bytes 2097184 | tf_op jit(solution)/shard_map/ppermute | solution.py:11
  139.5 7.7 %multiply_reduce_fusion = (f32[512]{0:T(512)S(1)}, bf16[512,2048]{1,0:T(8,128)(2,1)S(1)}, bf16[1,1,512,2048]{3,2,1,0:T(8,128)(2,1)}, bf16[1,1,512,2048]{3,2,1,0:T(8,128)(2,1)}) fusion(bf16[512,2048]{1,0:T(8,128)(2,1)} %collective-permute-done.1, f32[2,512,2048]{2,1,0:T(8,128)} %copy-done.2, s32[]{:T(128)S(6)} %select_n.74, ...), kind=kLoop, calls=%fused_computation.25 | loop fusion | flops 24116736 | bytes 16781316 | tf_op jit(solution)/shard_map/reduce_sum | solution.py:81
  147.4 0.6 dynamic-slice
  148.3 74.5 %all-reduce = f32[16,2,32]{2,1,0:T(2,128)S(1)} all-reduce(f32[16,2,32]{2,1,0:T(2,128)S(1)} %bitcast_select_fusion.2), channel_id=4, replica_groups=mesh['dp'=2,'expert'=4,'tensor'=4] {'expert','tensor'}, use_global_device_ids=true, to_apply=%region_4.5.clone | all-reduce | flops 1024 | bytes 8192
  222.8 1.2 dynamic-slice_bitcast_fusion
  224.0 4.1 %broadcast_select_fusion.1 = (bf16[512,2048]{1,0:T(8,128)(2,1)}, bf16[512,2048]{1,0:T(8,128)(2,1)}) fusion(bf16[512,2048]{1,0:T(8,128)(2,1)S(1)} %get-tuple-element.7, bf16[512,2048]{1,0:T(8,128)(2,1)} %collective-permute-done.2, pred[]{:T(512)S(6)} %eq.51), kind=kLoop, calls=%fused_computation.30 | loop fusion | flops 2097152 | bytes 8388609 | tf_op jit(solution)/shard_map/jit(_where)/select_n | solution.py:25
  228.1 0.4 copy-done.1
  228.5 18.7 %convert_bitcast_fusion = bf16[1,2048,3072]{2,1,0:T(8,128)(2,1)} fusion(bf16[1024,3072]{1,0:T(8,128)(2,1)S(1)} %bitcast.88, f32[1024]{0:T(1024)S(1)} %mul.59, bf16[512,2048]{1,0:T(8,128)(2,1)} %get-tuple-element.11, bf16[512,2048]{1,0:T(8,128)(2,1)} %get-tuple-element.10), kind=kOutput, calls=%fused_computation.4 | convolution fusion | flops 12909019136 | bytes 23072768 | tf_op jit(solution)/shard_map/dot_general | solution.py:73
  (27 shorter events, 1.7 us)
Async XLA Ops:
  7.2 102.0 %all-gather.5.cloned.1.call-start = ((), (), s32[]{:S(2)}) async-start(), calls=%async_computation | async-start | bytes 6684672 | tf_op jit(solution)/shard_map/all_gather | solution.py:35
  8.3 1.6 collective-permute-start
  113.8 18.0 %copy-start = (bf16[4,256,3072]{2,1,0:T(8,128)(2,1)}, bf16[4,256,3072]{2,1,0:T(8,128)(2,1)S(1)}, u32[]{:S(2)}) copy-start(bf16[4,256,3072]{2,1,0:T(8,128)(2,1)S(1)} %convolution_convert_fusion) | copy-start | bytes 18874372
  131.8 3.4 %copy-start.2 = (f32[2,512,2048]{2,1,0:T(8,128)}, f32[2,512,2048]{2,1,0:T(8,128)S(1)}, u32[]{:S(2)}) copy-start(f32[2,512,2048]{2,1,0:T(8,128)S(1)} %fusion.1) | copy-start | bytes 25165828
  135.2 4.3 %collective-permute-start.1 = (bf16[512,2048]{1,0:T(8,128)(2,1)S(1)}, bf16[512,2048]{1,0:T(8,128)(2,1)}, u32[]{:S(2)}, u32[]{:S(2)}) collective-permute-start(bf16[512,2048]{1,0:T(8,128)(2,1)S(1)} %fusion.16), channel_id=1, source_target_pairs={{0,16},{16,0},{1,17},{17,1},{2,18},{18,2},{3,19},{19,3},{4,20},{20... | collective-permute-start | bytes 6291464 | tf_op jit(solution)/shard_map/ppermute | solution.py:11
  139.5 7.9 %copy-start.3 = (u32[32]{0:T(128)S(1)}, u32[32]{0:T(128)}, u32[]{:S(2)}) copy-start(u32[32]{0:T(128)} %constant.50) | copy-start | bytes 388
  147.2 76.9 %collective-permute-start.2 = (bf16[512,2048]{1,0:T(8,128)(2,1)S(1)}, bf16[512,2048]{1,0:T(8,128)(2,1)}, u32[]{:S(2)}, u32[]{:S(2)}) collective-permute-start(bf16[512,2048]{1,0:T(8,128)(2,1)S(1)} %get-tuple-element.7), channel_id=1, source_target_pairs={{0,16},{16,0},{1,17},{17,1},{2,18},{18,2},{3,19},{19,3},{4,20},{20... | collective-permute-start | bytes 6291464 | tf_op jit(solution)/shard_map/ppermute | solution.py:11
  224.0 4.4 %copy-start.1 = (bf16[4,256,3072]{2,1,0:T(8,128)(2,1)S(1)}, bf16[4,256,3072]{2,1,0:T(8,128)(2,1)}, u32[]{:S(2)}) copy-start(bf16[4,256,3072]{2,1,0:T(8,128)(2,1)} %copy-done) | copy-start | bytes 18874372
Sparse Core Ops, SparseCore 0:
  11.9 97.2 all-gather.4

commit v2 on v1

--- a/solution.py
+++ b/solution.py
@@ -25,14 +25,19 @@
         return jnp.where(first, mine, other), jnp.where(first, other, mine)
 
     meta = jnp.concatenate([routes[0].T.astype(F32), route_weight[0].T.astype(F32)], axis=0)
-    meta = lax.all_gather(meta, ("dp", "expert", "tensor"), axis=0)
-    meta = meta.reshape(2, n, 4, tok)
+    meta = jnp.stack(ordered(meta, swap(meta)))
+    meta = jnp.broadcast_to(meta[None], (n, 2, 4, tok))
+    meta = lax.all_to_all(meta, ("expert", "tensor"), split_axis=0, concat_axis=0, tiled=True)
+    meta = jnp.swapaxes(meta, 0, 1)
 
     low, high = out_grad[0, :, :half], out_grad[0, :, half:]
     keep = jnp.where(first, low, high)
     other = swap(jnp.where(first, high, low))
     both = jnp.stack(ordered(keep, other))
-    tokens = lax.all_gather(both, ("expert", "tensor"), axis=1)
+    piece = half // 2
+    tokens_a = lax.all_gather(both[:, :, :piece], ("expert", "tensor"), axis=1)
+    later, tokens_a = lax.optimization_barrier((both[:, :, piece:], tokens_a))
+    tokens_b = lax.all_gather(later, ("expert", "tensor"), axis=1)
 
     hits = meta[:, :, :2] == expert.astype(F32)
     taken = jnp.any(hits, axis=2)
@@ -47,13 +52,23 @@
     eye = jnp.eye(group, dtype=bool)
     wide = place.reshape(2, n // group, group, cap, 1, tok) & eye[:, None, :, None]
     wide = wide.reshape(2 * n // group, group * cap, group * tok).astype(BF)
-    routed = lax.dot_general(
-        wide,
-        tokens.reshape(2 * n // group, group * tok, half),
-        (((2,), (1,)), ((0,), (0,))),
-        preferred_element_type=F32,
-    ).reshape(2 * rows, half)
-    routed = routed.astype(BF)
+
+    def put(tokens):
+        routed = lax.dot_general(
+            wide,
+            tokens.reshape(2 * n // group, group * tok, piece),
+            (((2,), (1,)), ((0,), (0,))),
+            preferred_element_type=F32,
+        ).reshape(2 * rows, piece)
+        return routed.astype(BF)
+
+    def times(routed, weight):
+        return lax.dot_general(
+            routed, weight, (((1,), (1,)), ((), ())), preferred_element_type=F32
+        )
+
+    routed_a, routed_b = put(tokens_a), put(tokens_b)
+    routed = jnp.concatenate([routed_a, routed_b], axis=1)
 
     gate = gate_pre[0, 0].astype(F32)
     upper = up_pre[0, 0].astype(F32)
@@ -63,9 +78,8 @@
     hidden = (act * upper).astype(BF)
     hidden_both = jnp.concatenate(ordered(hidden, swap(hidden)), axis=0)
 
-    back = lax.dot_general(
-        routed, down_weight[0], (((1,), (1,)), ((), ())), preferred_element_type=F32
-    ).reshape(2, rows, -1)
+    back = times(routed_a, down_weight[0, :, :piece]) + times(routed_b, down_weight[0, :, piece:])
+    back = back.reshape(2, rows, -1)
     sent = lax.dynamic_index_in_dim(back, 1 - me, 0, keepdims=False).astype(BF)
     back = lax.dynamic_index_in_dim(back, me, 0, keepdims=False) + swap(sent).astype(F32)
 
@@ -83,8 +97,8 @@
     my_hits = lax.dynamic_index_in_dim(hits, me, 0, keepdims=False)
     tok_score = jnp.sum(jnp.where(my_place, score, 0.0), axis=1)
     pair = jnp.where(my_hits, tok_score[:, None, :], 0.0)
-    pair = lax.psum_scatter(pair, ("expert", "tensor"), scatter_dimension=0, tiled=True)
-    route_grad = pair.reshape(2, tok).T[None]
+    pair = lax.all_to_all(pair, ("expert", "tensor"), split_axis=0, concat_axis=0, tiled=True)
+    route_grad = jnp.sum(pair, axis=0).T[None]
     return (route_grad, gate_grad[None, None], up_grad[None, None], down_grad[None])
 
 

time: 254 us -> 234 us (0.921)
  blocking collectives: 146 us -> 0 us
  waiting for transfers between devices: 25.9 us -> 139 us
  starting transfers between devices: 0.7 us -> 9.11 us
  matrix products: 41.3 us -> 44.4 us
    all_gather x1 -> x2, waiting for transfers between devices: 20.8 us -> 119 us  [the longest x1 70.9 us: shards(): tokens_a = lax.all_gather(both[:, :, :piece], ('expert', 'tensor'), axis=1)]
    unnamed x1 -> x0, blocking collectives: 74.5 us -> none
    all_gather x1 -> x0, blocking collectives: 71.7 us -> none  [shards(): meta = lax.all_gather(meta, ('dp', 'expert', 'tensor'), axis=0)]
    all_to_all x0 -> x2, waiting for transfers between devices: none -> 14 us  [the longest x1 7.23 us: shards(): lax.all_to_all(pair, ('expert', 'tensor'), split_axis=0, concat_axis=0, t...]
    all_to_all x0 -> x2, starting transfers between devices: none -> 8.23 us  [the longest x1 4.13 us: shards(): lax.all_to_all(pair, ('expert', 'tensor'), split_axis=0, concat_axis=0, t...]
    dot_general x2 -> x4, matrix products: 22.6 us -> 24.7 us  [the longest x2 18.9 us: times(): lax.dot_general(routed, weight, (((1,), (1,)), ((), ())), preferred_eleme...]
    ppermute x3 -> x4, waiting for transfers between devices: 5.05 us -> 6.16 us  [swap(): return lax.ppermute(x, 'dp', [(0, 1), (1, 0)])]
  transfers between devices with their start and end apart: 4 -> 8, of which waited for: 3 -> 7; matrix products, arithmetic and copies ran while one was open for 3% -> 5% of each run, Pallas kernels for 0% -> 0%
where the time goes in v2:
time: 234 us
  waiting for transfers between devices  139 us (59%)
  matrix products  44.4 us (19%)
  other arithmetic  19.2 us (8%)
  between operations  14.3 us (6%)
  starting transfers between devices  9.11 us (4%)
  local copies, waits for them, and re-layouts  7.93 us (3%)
    all_gather x1, waiting for transfers between devices, shards(): tokens_a = lax.all_gather(both[:, :, :piece], ('expert', 'tensor'), axis=1)  70.9 us
    all_gather x1, waiting for transfers between devices, shards(): tokens_b = lax.all_gather(later, ('expert', 'tensor'), axis=1)  47.9 us
    dot_general x1, matrix products, shards(): lax.dot_general(hidden_both, scaled, (((0,), (0,)), ((), ())), preferred_...  19.7 us
    dot_general x2, matrix products, times(): lax.dot_general(routed, weight, (((1,), (1,)), ((), ())), preferred_eleme...  18.9 us
    reduce_sum x1, other arithmetic, shards(): score = jnp.sum(hidden.astype(F32) * back, axis=1).reshape(n, cap, 1)  7.68 us
    all_to_all x1, waiting for transfers between devices, shards(): lax.all_to_all(pair, ('expert', 'tensor'), split_axis=0, concat_axis=0, t...  7.23 us
    all_to_all x1, waiting for transfers between devices, shards(): lax.all_to_all(meta, ('expert', 'tensor'), split_axis=0, concat_axis=0, t...  6.75 us
    ppermute x4, waiting for transfers between devices, swap(): return lax.ppermute(x, 'dp', [(0, 1), (1, 0)])  6.16 us
  transfers between devices with their start and end apart: 8, of which 7 were waited for; matrix products, arithmetic and copies ran while one was open for 5% of the time, Pallas kernels for 0%

profile of v2, /device:TPU:0, one launch (start us, length us, event | category | flops | bytes accessed | tf_op | source)
XLA Modules:
  0.0 233.9 jit_solution(3694256639691073226)
XLA Ops:
  7.2 1.0 select_bitcast_fusion
  8.8 1.1 collective-permute-done.1
  9.9 1.1 fusion.35
  10.9 0.8 pad_maximum_fusion
  11.8 70.9 %all-gather.5.cloned.1.call-done = bf16[2,512,1536]{2,1,0:T(8,128)(2,1)} async-done(((bf16[2,32,1536]{2,1,0:T(8,128)(2,1)}), bf16[2,512,1536]{2,1,0:T(8,128)(2,1)}) %all-gather.5.cloned.1.call-update) | async-done | bytes 3145744 | tf_op jit(solution)/shard_map/all_gather | solution.py:38
  83.3 0.7 convert_bitcast_fusion.2
  84.1 1.1 collective-permute-done
  85.3 0.7 reshape.85
  86.0 4.1 %all-to-all-start = ((f32[16,1,256]{2,1,0:T(1,128)}), f32[16,1,256]{2,1,0:T(1,128)S(1)}, u32[]{:S(2)}, u32[]{:S(2)}) async-start(f32[16,1,256]{2,1,0:T(1,128)} %reshape.85), calls=%async_computation | async-start | bytes 32768 | tf_op jit(solution)/shard_map/all_to_all | solution.py:30
  90.7 6.7 %all-to-all-done = f32[16,1,256]{2,1,0:T(1,128)S(1)} async-done(((f32[16,1,256]{2,1,0:T(1,128)}), f32[16,1,256]{2,1,0:T(1,128)S(1)}, u32[]{:S(2)}, u32[]{:S(2)}) %all-to-all-start) | async-done | bytes 16416 | tf_op jit(solution)/shard_map/all_to_all | solution.py:30
  97.9 0.7 reduce
  100.2 1.5 and.59
  101.8 2.9 %convolution_convert_fusion.1 = bf16[4,256,1536]{2,1,0:T(8,128)(2,1)S(1)} fusion(bf16[4,256,1536]{2,1,0:T(8,128)(2,1)} %bitcast.97, pred[4,256,256]{2,1,0:T(32,128)(4,1)S(1)} %and.59, pred[256,256]{1,0:T(8,128)(4,1)S(1)} %and.61), kind=kOutput, calls=%fused_computation.34 | convolution fusion | flops 807141376 | bytes 6619136 | tf_op jit(solution)/shard_map/dot_general | solution.py:57
  104.7 47.9 %all-gather.7.cloned.1.call-done = bf16[2,512,1536]{2,1,0:T(8,128)(2,1)} async-done(((bf16[2,32,1536]{2,1,0:T(8,128)(2,1)}), bf16[2,512,1536]{2,1,0:T(8,128)(2,1)}) %all-gather.7.cloned.1.call-update) | async-done | bytes 3145744 | tf_op jit(solution)/shard_map/all_gather | solution.py:40
  152.6 2.9 %convolution_convert_fusion = bf16[4,256,1536]{2,1,0:T(8,128)(2,1)S(1)} fusion(bf16[4,256,1536]{2,1,0:T(8,128)(2,1)} %bitcast.100, pred[4,256,256]{2,1,0:T(32,128)(4,1)S(1)} %and.59, pred[256,256]{1,0:T(8,128)(4,1)S(1)} %and.61), kind=kOutput, calls=%fused_computation.33 | convolution fusion | flops 807141376 | bytes 6619136 | tf_op jit(solution)/shard_map/dot_general | solution.py:57
  155.4 9.9 %fusion.3 = f32[1024,2048]{1,0:T(8,128)S(1)} fusion(bf16[1024,1536]{1,0:T(8,128)(2,1)S(1)} %bitcast.101, bf16[1,2048,3072]{2,1,0:T(8,128)(2,1)} %param.11), kind=kOutput, calls=%fused_computation.5 | convolution fusion | flops 6442450944 | bytes 17825792 | tf_op jit(solution)/shard_map/dot_general | solution.py:66
  165.4 9.0 %fusion.21 = f32[1024,2048]{1,0:T(8,128)S(1)} fusion(f32[1024,2048]{1,0:T(8,128)S(1)} %fusion.3, bf16[1024,1536]{1,0:T(8,128)(2,1)S(1)} %bitcast.98, bf16[1,2048,3072]{2,1,0:T(8,128)(2,1)} %param.11), kind=kOutput, calls=%fused_computation.32 | convolution fusion | flops 6444548096 | bytes 26214400 | tf_op jit(solution)/shard_map/dot_general | solution.py:66
  174.4 3.4 %copy-done = f32[1024,2048]{1,0:T(8,128)} copy-done((f32[1024,2048]{1,0:T(8,128)}, f32[1024,2048]{1,0:T(8,128)S(1)}, u32[]{:S(2)}) %copy-start) | copy-done | bytes 8388632
  178.5 4.0 %collective-permute-done.2 = bf16[512,2048]{1,0:T(8,128)(2,1)} collective-permute-done((bf16[512,2048]{1,0:T(8,128)(2,1)S(1)}, bf16[512,2048]{1,0:T(8,128)(2,1)}, u32[]{:S(2)}, u32[]{:S(2)}) %collective-permute-start.2) | collective-permute-done | bytes 2097184 | tf_op jit(solution)/shard_map/ppermute | solution.py:11
  182.5 7.7 %multiply_reduce_fusion = (f32[512]{0:T(512)S(1)}, bf16[512,2048]{1,0:T(8,128)(2,1)S(1)}, bf16[1,1,512,2048]{3,2,1,0:T(8,128)(2,1)}, bf16[1,1,512,2048]{3,2,1,0:T(8,128)(2,1)}) fusion(bf16[512,2048]{1,0:T(8,128)(2,1)} %collective-permute-done.2, f32[2,512,2048]{2,1,0:T(8,128)} %bitcast.96, s32[]{:T(128)S(6)} %select_n.89, ...), kind=kLoop, calls=%fused_computation.30 | loop fusion | flops 24116736 | bytes 16781316 | tf_op jit(solution)/shard_map/reduce_sum | solution.py:95
  191.3 4.1 %all-to-all-start.1 = ((f32[16,2,32]{2,1,0:T(2,128)}), f32[16,2,32]{2,1,0:T(2,128)S(1)}, u32[]{:S(2)}, u32[]{:S(2)}) async-start(f32[16,2,32]{2,1,0:T(2,128)} %bitcast_select_fusion.2), calls=%async_computation.1 | async-start | bytes 32768 | tf_op jit(solution)/shard_map/all_to_all | solution.py:100
  195.5 7.2 %all-to-all-done.1 = f32[16,2,32]{2,1,0:T(2,128)S(1)} async-done(((f32[16,2,32]{2,1,0:T(2,128)}), f32[16,2,32]{2,1,0:T(2,128)S(1)}, u32[]{:S(2)}, u32[]{:S(2)}) %all-to-all-start.1) | async-done | bytes 4128 | tf_op jit(solution)/shard_map/all_to_all | solution.py:100
  203.3 4.0 %broadcast_select_fusion.1 = (bf16[512,2048]{1,0:T(8,128)(2,1)}, bf16[512,2048]{1,0:T(8,128)(2,1)}) fusion(bf16[512,2048]{1,0:T(8,128)(2,1)S(1)} %get-tuple-element.11, bf16[512,2048]{1,0:T(8,128)(2,1)} %collective-permute-done.3, pred[]{:T(512)S(6)} %eq.41), kind=kLoop, calls=%fused_computation.38 | loop fusion | flops 2097152 | bytes 8388609 | tf_op jit(solution)/shard_map/jit(_where)/select_n | solution.py:25
  207.3 19.7 %convert_bitcast_fusion = bf16[1,2048,3072]{2,1,0:T(8,128)(2,1)} fusion(bf16[1024,1536]{1,0:T(8,128)(2,1)} %bitcast.102, bf16[1024,1536]{1,0:T(8,128)(2,1)S(1)} %bitcast.99, f32[1024]{0:T(1024)S(1)} %mul.59, bf16[512,2048]{1,0:T(8,128)(2,1)} %get-tuple-element.15, bf16[512,2048]{1,0:T(8,128)(2,1)} %get-tuple-element.14), kind=kOutput, calls=%fused_computation | convolution fusion | flops 12918456320 | bytes 23072768 | tf_op jit(solution)/shard_map/dot_general | solution.py:87
  (45 shorter events, 6.5 us)
Async XLA Ops:
  7.2 75.5 %all-gather.5.cloned.1.call-start = ((), (), s32[]{:S(2)}) async-start(), calls=%async_computation.2 | async-start | bytes 3342336 | tf_op jit(solution)/shard_map/all_gather | solution.py:38
  8.3 1.6 collective-permute-start.1
  11.7 140.8 %all-gather.7.cloned.1.call-start = ((), (), s32[]{:S(2)}) async-start(), calls=%async_computation.3 | async-start | bytes 3342336 | tf_op jit(solution)/shard_map/all_gather | solution.py:40
  84.0 1.2 collective-permute-start
  86.0 11.4 %all-to-all-start = ((f32[16,1,256]{2,1,0:T(1,128)}), f32[16,1,256]{2,1,0:T(1,128)S(1)}, u32[]{:S(2)}, u32[]{:S(2)}) async-start(f32[16,1,256]{2,1,0:T(1,128)} %reshape.85), calls=%async_computation | async-start | bytes 32768 | tf_op jit(solution)/shard_map/all_to_all | solution.py:30
  104.6 60.8 %copy-start.1 = (bf16[4,256,1536]{2,1,0:T(8,128)(2,1)}, bf16[4,256,1536]{2,1,0:T(8,128)(2,1)S(1)}, u32[]{:S(2)}) copy-start(bf16[4,256,1536]{2,1,0:T(8,128)(2,1)S(1)} %convolution_convert_fusion.1) | copy-start | bytes 9437188
  155.4 10.0 %copy-start.3 = (bf16[4,256,1536]{2,1,0:T(8,128)(2,1)}, bf16[4,256,1536]{2,1,0:T(8,128)(2,1)S(1)}, u32[]{:S(2)}) copy-start(bf16[4,256,1536]{2,1,0:T(8,128)(2,1)S(1)} %convolution_convert_fusion) | copy-start | bytes 9437188
  174.4 3.4 %copy-start = (f32[1024,2048]{1,0:T(8,128)}, f32[1024,2048]{1,0:T(8,128)S(1)}, u32[]{:S(2)}) copy-start(f32[1024,2048]{1,0:T(8,128)S(1)} %fusion.21) | copy-start | bytes 25165828
  178.1 4.4 %collective-permute-start.2 = (bf16[512,2048]{1,0:T(8,128)(2,1)S(1)}, bf16[512,2048]{1,0:T(8,128)(2,1)}, u32[]{:S(2)}, u32[]{:S(2)}) collective-permute-start(bf16[512,2048]{1,0:T(8,128)(2,1)S(1)} %fusion.24), channel_id=1, source_target_pairs={{0,16},{16,0},{1,17},{17,1},{2,18},{18,2},{3,19},{19,3},{4,20},{20... | collective-permute-start | bytes 6291464 | tf_op jit(solution)/shard_map/ppermute | solution.py:11
  190.2 13.1 %collective-permute-start.3 = (bf16[512,2048]{1,0:T(8,128)(2,1)S(1)}, bf16[512,2048]{1,0:T(8,128)(2,1)}, u32[]{:S(2)}, u32[]{:S(2)}) collective-permute-start(bf16[512,2048]{1,0:T(8,128)(2,1)S(1)} %get-tuple-element.11), channel_id=1, source_target_pairs={{0,16},{16,0},{1,17},{17,1},{2,18},{18,2},{3,19},{19,3},{4,20},{20... | collective-permute-start | bytes 6291464 | tf_op jit(solution)/shard_map/ppermute | solution.py:11
  191.3 11.4 %all-to-all-start.1 = ((f32[16,2,32]{2,1,0:T(2,128)}), f32[16,2,32]{2,1,0:T(2,128)S(1)}, u32[]{:S(2)}, u32[]{:S(2)}) async-start(f32[16,2,32]{2,1,0:T(2,128)} %bitcast_select_fusion.2), calls=%async_computation.1 | async-start | bytes 32768 | tf_op jit(solution)/shard_map/all_to_all | solution.py:100
  203.3 4.1 %copy-start.2 = (bf16[4,256,1536]{2,1,0:T(8,128)(2,1)S(1)}, bf16[4,256,1536]{2,1,0:T(8,128)(2,1)}, u32[]{:S(2)}) copy-start(bf16[4,256,1536]{2,1,0:T(8,128)(2,1)} %copy-done.1) | copy-start | bytes 9437188
Sparse Core Ops, SparseCore 0:
  11.8 70.7 all-gather.4
  85.9 66.6 all-gather.6

commit v3 on v1

--- a/solution.py
+++ b/solution.py
@@ -1,6 +1,10 @@
+import functools
+
 import jax
 import jax.numpy as jnp
 from jax import lax
+from jax.experimental import pallas as pl
+from jax.experimental.pallas import tpu as pltpu
 from jax.sharding import PartitionSpec as P
 
 BF = jnp.bfloat16
@@ -9,6 +13,137 @@
 
 def swap(x):
     return lax.ppermute(x, "dp", [(0, 1), (1, 0)])
+
+
+def gather_kernel(experts, depth, own_ref, out_ref, own_sem, recv_sem, send_sem, x_sem, y_sem):
+    expert = lax.axis_index("expert")
+    level = lax.axis_index("tensor")
+    others = experts // 2 - 1
+    a, b = expert // 2, lax.rem(expert, 2)
+    x_expert = a * 2 + 1 - b
+    y_experts = [lax.rem(a + j, others + 1) * 2 + b for j in range(1, others + 1)]
+    partner = {"expert": x_expert, "tensor": level}
+    across = [{"expert": e, "tensor": level} for e in y_experts]
+    above = {"expert": expert, "tensor": level + 1}
+    below = {"expert": expert, "tensor": level - 1}
+    has_above, has_below = level < depth - 1, level > 0
+
+    barrier = pltpu.get_barrier_semaphore()
+
+    def greet(target):
+        pl.semaphore_signal(barrier, inc=1, device_id=target, device_id_type=pl.DeviceIdType.MESH)
+
+    for target in [partner] + across:
+        greet(target)
+    pl.when(has_above)(lambda: greet(above))
+    pl.when(has_below)(lambda: greet(below))
+    ends = jnp.where(has_above, 1, 0) + jnp.where(has_below, 1, 0)
+    pl.semaphore_wait(barrier, 1 + others + ends)
+
+    def copy(h, block, target, sem, own=False):
+        return pltpu.make_async_remote_copy(
+            src_ref=own_ref.at[h] if own else out_ref.at[h, block],
+            dst_ref=out_ref.at[h, block],
+            send_sem=sem,
+            recv_sem=recv_sem.at[h, block],
+            device_id=target,
+            device_id_type=pl.DeviceIdType.MESH,
+        )
+
+    def arrived(h, block):
+        copy(h, block, partner, send_sem.at[0, 0, 0]).wait_recv()
+
+    def column(k, up, act):
+        t = level - k if up else level + k
+        block = expert * depth + t
+        own = k == 0
+
+        def go():
+            for h in range(2):
+                if act == "start" and not own:
+                    arrived(h, block)
+                todo = []
+                if own or up:
+                    todo.append((has_above, above, 0))
+                if own or not up:
+                    todo.append((has_below, below, 1))
+                todo.append((None, partner, 2))
+                todo += [(None, target, 3 + j) for j, target in enumerate(across)]
+                for when, target, kind in todo:
+                    one = copy(h, block, target, send_sem.at[h, t, kind], own)
+                    run = one.start if act == "start" else one.wait_send
+                    if when is None:
+                        run()
+                    else:
+                        pl.when(when)(run)
+
+        pl.when(t >= 0 if up else t < depth)(go)
+
+    def cross(k, up, act):
+        t = level - k if up else level + k
+
+        def go():
+            block = x_expert * depth + t
+            if act == "start":
+                arrived(0, block)
+            for j, target in enumerate(across):
+                one = copy(0, block, target, x_sem.at[t, j])
+                one.start() if act == "start" else one.wait_send()
+            for j, e in enumerate(y_experts):
+                if act == "start":
+                    arrived(1, e * depth + t)
+                one = copy(1, e * depth + t, partner, y_sem.at[t, j])
+                one.start() if act == "start" else one.wait_send()
+
+        pl.when(t >= 0 if up else t < depth)(go)
+
+    mine = expert * depth + level
+    keeps = [
+        pltpu.make_async_copy(own_ref.at[h], out_ref.at[h, mine], own_sem.at[h]) for h in range(2)
+    ]
+    for keep in keeps:
+        keep.start()
+    sides = lambda k: (True,) if k == 0 else (True, False)
+    for k in range(depth + 1):
+        if k < depth:
+            for up in sides(k):
+                column(k, up, "start")
+        if k > 0:
+            for up in sides(k - 1):
+                cross(k - 1, up, "start")
+    for t in range(depth):
+        arrived(1, x_expert * depth + t)
+        for e in y_experts:
+            arrived(0, e * depth + t)
+            far = e + 1 - 2 * b
+            arrived(0, far * depth + t)
+            arrived(1, far * depth + t)
+    for k in range(depth):
+        for up in sides(k):
+            column(k, up, "end")
+            cross(k, up, "end")
+    for keep in keeps:
+        keep.wait()
+
+
+def gather(own):
+    experts, depth = lax.axis_size("expert"), lax.axis_size("tensor")
+    others = experts // 2 - 1
+    n = experts * depth
+    return pl.pallas_call(
+        functools.partial(gather_kernel, experts, depth),
+        out_shape=jax.ShapeDtypeStruct((2, n) + own.shape[1:], own.dtype),
+        in_specs=[pl.BlockSpec(memory_space=pl.ANY)],
+        out_specs=pl.BlockSpec(memory_space=pl.ANY),
+        scratch_shapes=[
+            pltpu.SemaphoreType.DMA((2,)),
+            pltpu.SemaphoreType.DMA((2, n)),
+            pltpu.SemaphoreType.DMA((2, depth, 3 + others)),
+            pltpu.SemaphoreType.DMA((depth, others)),
+            pltpu.SemaphoreType.DMA((depth, others)),
+        ],
+        compiler_params=pltpu.CompilerParams(collective_id=0, has_side_effects=True),
+    )(own)
 
 
 def shards(out_grad, routes, route_weight, gate_pre, up_pre, down_weight):
@@ -24,15 +159,15 @@
     def ordered(mine, other):
         return jnp.where(first, mine, other), jnp.where(first, other, mine)
 
-    meta = jnp.concatenate([routes[0].T.astype(F32), route_weight[0].T.astype(F32)], axis=0)
-    meta = lax.all_gather(meta, ("dp", "expert", "tensor"), axis=0)
-    meta = meta.reshape(2, n, 4, tok)
-
-    low, high = out_grad[0, :, :half], out_grad[0, :, half:]
+    meta = jnp.concatenate([routes[0].astype(BF), route_weight[0]], axis=1)
+    meta = jnp.pad(meta, ((0, 0), (0, 124)))
+    low = jnp.concatenate([out_grad[0, :, :half], meta], axis=1)
+    high = jnp.concatenate([out_grad[0, :, half:], meta], axis=1)
     keep = jnp.where(first, low, high)
     other = swap(jnp.where(first, high, low))
-    both = jnp.stack(ordered(keep, other))
-    tokens = lax.all_gather(both, ("expert", "tensor"), axis=1)
+    both = gather(jnp.stack(ordered(keep, other)))
+    tokens = both[..., :half]
+    meta = jnp.swapaxes(both[..., half : half + 4].astype(F32), 2, 3)
 
     hits = meta[:, :, :2] == expert.astype(F32)
     taken = jnp.any(hits, axis=2)
@@ -47,6 +182,7 @@
     eye = jnp.eye(group, dtype=bool)
     wide = place.reshape(2, n // group, group, cap, 1, tok) & eye[:, None, :, None]
     wide = wide.reshape(2 * n // group, group * cap, group * tok).astype(BF)
+
     routed = lax.dot_general(
         wide,
         tokens.reshape(2 * n // group, group * tok, half),
@@ -83,8 +219,8 @@
     my_hits = lax.dynamic_index_in_dim(hits, me, 0, keepdims=False)
     tok_score = jnp.sum(jnp.where(my_place, score, 0.0), axis=1)
     pair = jnp.where(my_hits, tok_score[:, None, :], 0.0)
-    pair = lax.psum_scatter(pair, ("expert", "tensor"), scatter_dimension=0, tiled=True)
-    route_grad = pair.reshape(2, tok).T[None]
+    pair = lax.all_to_all(pair, ("expert", "tensor"), split_axis=0, concat_axis=0, tiled=True)
+    route_grad = jnp.sum(pair, axis=0).T[None]
     return (route_grad, gate_grad[None, None], up_grad[None, None], down_grad[None])
 
 

time: 254 us -> 152 us (0.60)
  blocking collectives: 146 us -> 0 us
  Pallas kernels: 0 us -> 59 us
  waiting for transfers between devices: 25.9 us -> 11.7 us
  between operations: 14.2 us -> 0.81 us
  local copies, waits for them, and re-layouts: 8.44 us -> 15.5 us
  starting transfers between devices: 0.7 us -> 6.49 us
    unnamed x1 -> x0, blocking collectives: 74.5 us -> none
    all_gather x1 -> x0, blocking collectives: 71.7 us -> none  [shards(): meta = lax.all_gather(meta, ('dp', 'expert', 'tensor'), axis=0)]
    pallas_call x0 -> x1, Pallas kernels: none -> 59 us  [gather(): pl.pallas_call(functools.partial(gather_kernel, experts, depth), out_shap...]
    all_gather x1 -> x0, waiting for transfers between devices: 20.8 us -> none  [shards(): tokens = lax.all_gather(both, ('expert', 'tensor'), axis=1)]
    all_to_all x0 -> x1, waiting for transfers between devices: none -> 7.23 us  [shards(): lax.all_to_all(pair, ('expert', 'tensor'), split_axis=0, concat_axis=0, t...]
    slice x0 -> x1, local copies, waits for them, and re-layouts: none -> 6.21 us  [shards(): tokens = both[..., :half]]
    all_to_all x0 -> x1, starting transfers between devices: none -> 5.83 us  [shards(): lax.all_to_all(pair, ('expert', 'tensor'), split_axis=0, concat_axis=0, t...]
  transfers between devices with their start and end apart: 4 -> 4, of which waited for: 3 -> 3; matrix products, arithmetic and copies ran while one was open for 3% -> 2% of each run, Pallas kernels for 0% -> 0%
where the time goes in v3:
time: 152 us
  Pallas kernels  59 us (39%)
  matrix products  41.3 us (27%)
  other arithmetic  17.3 us (11%)
  local copies, waits for them, and re-layouts  15.5 us (10%)
  waiting for transfers between devices  11.7 us (8%)
  starting transfers between devices  6.49 us (4%)
    pallas_call x1, Pallas kernels, gather(): pl.pallas_call(functools.partial(gather_kernel, experts, depth), out_shap...  59 us
    dot_general x1, matrix products, shards(): lax.dot_general(hidden_both, scaled, (((0,), (0,)), ((), ())), preferred_...  18.7 us
    dot_general x1, matrix products, shards(): lax.dot_general(routed, down_weight[0], (((1,), (1,)), ((), ())), preferr...  18 us
    reduce_sum x1, other arithmetic, shards(): score = jnp.sum(hidden.astype(F32) * back, axis=1).reshape(n, cap, 1)  7.68 us
    all_to_all x1, waiting for transfers between devices, shards(): lax.all_to_all(pair, ('expert', 'tensor'), split_axis=0, concat_axis=0, t...  7.23 us
    slice x1, local copies, waits for them, and re-layouts, shards(): tokens = both[..., :half]  6.21 us
    all_to_all x1, starting transfers between devices, shards(): lax.all_to_all(pair, ('expert', 'tensor'), split_axis=0, concat_axis=0, t...  5.83 us
    dot_general x1, matrix products, shards(): lax.dot_general(wide, tokens.reshape(2 * n // group, group * tok, half),...  4.59 us
  transfers between devices with their start and end apart: 4, of which 3 were waited for; matrix products, arithmetic and copies ran while one was open for 2% of the time, Pallas kernels for 0%

profile of v3, /device:TPU:0, one launch (start us, length us, event | category | flops | bytes accessed | tf_op | source)
XLA Modules:
  0.0 152.1 jit_solution(16993379974484102407)
XLA Ops:
  0.6 0.7 convert_bitcast_fusion.2
  1.3 0.7 pad_maximum_fusion.1
  2.1 1.0 slice_bitcast_fusion.1
  3.2 0.5 collective-permute-start
  4.3 0.5 collective-permute-done
  4.9 0.8 pad_maximum_fusion.own_ref
  5.7 59.0 %shard_map.93 = bf16[2,16,32,3200]{3,2,1,0:T(8,128)(2,1)} custom-call(bf16[2,32,3200]{2,1,0:T(8,128)(2,1)} %pad_maximum_fusion.own_ref), custom_call_target="tpu_custom_call" | custom-call | tf_op jit(solution)/shard_map/pallas_call | solution.py:133
  64.7 1.0 convert_bitcast_fusion.1
  65.7 6.2 %slice.22 = bf16[2,16,32,3072]{3,2,1,0:T(8,128)(2,1)} slice(bf16[2,16,32,3200]{3,2,1,0:T(8,128)(2,1)} %shard_map.93), slice={[0:2], [0:16], [0:32], [0:3072]} | slice | bytes 12582912 | tf_op jit(solution)/shard_map/slice | solution.py:169
  72.3 0.6 reduce_or.9
  72.9 0.6 select_reduce_fusion.1
  73.6 0.6 and.58
  74.2 1.5 and.59
  75.8 4.6 %convolution_convert_fusion = bf16[4,256,3072]{2,1,0:T(8,128)(2,1)S(1)} fusion(bf16[4,256,3072]{2,1,0:T(8,128)(2,1)} %bitcast.70, pred[4,256,256]{2,1,0:T(32,128)(4,1)S(1)} %and.59, pred[256,256]{1,0:T(8,128)(4,1)S(1)} %and.61), kind=kOutput, calls=%fused_computation.9 | convolution fusion | flops 1614020608 | bytes 12910592 | tf_op jit(solution)/shard_map/dot_general | solution.py:186
  80.4 18.0 %fusion.1 = f32[2,512,2048]{2,1,0:T(8,128)S(1)} fusion(bf16[2,512,3072]{2,1,0:T(8,128)(2,1)S(1)} %bitcast.71, bf16[1,2048,3072]{2,1,0:T(8,128)(2,1)} %param.11), kind=kOutput, calls=%fused_computation.2 | convolution fusion | flops 12884901888 | bytes 27262976 | tf_op jit(solution)/shard_map/dot_general | solution.py:202
  98.7 3.1 %copy-done.2 = f32[2,512,2048]{2,1,0:T(8,128)} copy-done((f32[2,512,2048]{2,1,0:T(8,128)}, f32[2,512,2048]{2,1,0:T(8,128)S(1)}, u32[]{:S(2)}) %copy-start.2) | copy-done | bytes 8388632
  102.1 4.0 %collective-permute-done.1 = bf16[512,2048]{1,0:T(8,128)(2,1)} collective-permute-done((bf16[512,2048]{1,0:T(8,128)(2,1)S(1)}, bf16[512,2048]{1,0:T(8,128)(2,1)}, u32[]{:S(2)}, u32[]{:S(2)}) %collective-permute-start.1) | collective-permute-done | bytes 2097184 | tf_op jit(solution)/shard_map/ppermute | solution.py:15
  106.1 7.7 %multiply_reduce_fusion = (f32[512]{0:T(512)S(1)}, bf16[512,2048]{1,0:T(8,128)(2,1)S(1)}, bf16[1,1,512,2048]{3,2,1,0:T(8,128)(2,1)}, bf16[1,1,512,2048]{3,2,1,0:T(8,128)(2,1)}) fusion(bf16[512,2048]{1,0:T(8,128)(2,1)} %collective-permute-done.1, f32[2,512,2048]{2,1,0:T(8,128)} %copy-done.2, s32[]{:T(128)S(6)} %select_n.71, ...), kind=kLoop, calls=%fused_computation.25 | loop fusion | flops 24116736 | bytes 16781316 | tf_op jit(solution)/shard_map/reduce_sum | solution.py:217
  114.4 0.6 copy.22
  115.0 5.8 %all-to-all-start = ((f32[16,2,32]{2,1,0:T(2,128)}), f32[16,2,32]{2,1,0:T(2,128)S(1)}, u32[]{:S(2)}, u32[]{:S(2)}) async-start(f32[16,2,32]{2,1,0:T(2,128)} %copy.22), calls=%async_computation | async-start | bytes 32768 | tf_op jit(solution)/shard_map/all_to_all | solution.py:222
  121.0 7.2 %all-to-all-done = f32[16,2,32]{2,1,0:T(2,128)S(1)} async-done(((f32[16,2,32]{2,1,0:T(2,128)}), f32[16,2,32]{2,1,0:T(2,128)S(1)}, u32[]{:S(2)}, u32[]{:S(2)}) %all-to-all-start) | async-done | bytes 4128 | tf_op jit(solution)/shard_map/all_to_all | solution.py:222
  128.3 0.6 copy.24
  128.9 4.1 %broadcast_select_fusion.1 = (bf16[512,2048]{1,0:T(8,128)(2,1)}, bf16[512,2048]{1,0:T(8,128)(2,1)}) fusion(bf16[512,2048]{1,0:T(8,128)(2,1)S(1)} %get-tuple-element.7, bf16[512,2048]{1,0:T(8,128)(2,1)} %collective-permute-done.2, pred[]{:T(512)S(6)} %eq.41), kind=kLoop, calls=%fused_computation.30 | loop fusion | flops 2097152 | bytes 8388609 | tf_op jit(solution)/shard_map/jit(_where)/select_n | solution.py:160
  133.4 18.7 %convert_bitcast_fusion = bf16[1,2048,3072]{2,1,0:T(8,128)(2,1)} fusion(bf16[1024,3072]{1,0:T(8,128)(2,1)S(1)} %bitcast.72, f32[1024]{0:T(1024)S(1)} %mul.59, bf16[512,2048]{1,0:T(8,128)(2,1)} %get-tuple-element.11, bf16[512,2048]{1,0:T(8,128)(2,1)} %get-tuple-element.10), kind=kOutput, calls=%fused_computation.4 | convolution fusion | flops 12909019136 | bytes 23072768 | tf_op jit(solution)/shard_map/dot_general | solution.py:209
  (30 shorter events, 3.2 us)
Async XLA Ops:
  3.2 1.6 %collective-permute-start = (bf16[32,3200]{1,0:T(8,128)(2,1)S(1)}, bf16[32,3200]{1,0:T(8,128)(2,1)S(1)}, u32[]{:S(2)}, u32[]{:S(2)}) collective-permute-start(bf16[32,3200]{1,0:T(8,128)(2,1)S(1)} %broadcast_select_fusion.2), channel_id=1, source_target_pairs={{0,16},{16,0},{1,17},{17,1},{2,18},{18,2},{3,19},{19,3},{4,20},{20... | collective-permute-start | bytes 614408 | tf_op jit(solution)/shard_map/ppermute | solution.py:15
  80.4 18.0 %copy-start = (bf16[4,256,3072]{2,1,0:T(8,128)(2,1)}, bf16[4,256,3072]{2,1,0:T(8,128)(2,1)S(1)}, u32[]{:S(2)}) copy-start(bf16[4,256,3072]{2,1,0:T(8,128)(2,1)S(1)} %convolution_convert_fusion) | copy-start | bytes 18874372
  98.4 3.4 %copy-start.2 = (f32[2,512,2048]{2,1,0:T(8,128)}, f32[2,512,2048]{2,1,0:T(8,128)S(1)}, u32[]{:S(2)}) copy-start(f32[2,512,2048]{2,1,0:T(8,128)S(1)} %fusion.1) | copy-start | bytes 25165828
  101.8 4.3 %collective-permute-start.1 = (bf16[512,2048]{1,0:T(8,128)(2,1)S(1)}, bf16[512,2048]{1,0:T(8,128)(2,1)}, u32[]{:S(2)}, u32[]{:S(2)}) collective-permute-start(bf16[512,2048]{1,0:T(8,128)(2,1)S(1)} %fusion.16), channel_id=1, source_target_pairs={{0,16},{16,0},{1,17},{17,1},{2,18},{18,2},{3,19},{19,3},{4,20},{20... | collective-permute-start | bytes 6291464 | tf_op jit(solution)/shard_map/ppermute | solution.py:15
  113.7 15.2 %collective-permute-start.2 = (bf16[512,2048]{1,0:T(8,128)(2,1)S(1)}, bf16[512,2048]{1,0:T(8,128)(2,1)}, u32[]{:S(2)}, u32[]{:S(2)}) collective-permute-start(bf16[512,2048]{1,0:T(8,128)(2,1)S(1)} %get-tuple-element.7), channel_id=1, source_target_pairs={{0,16},{16,0},{1,17},{17,1},{2,18},{18,2},{3,19},{19,3},{4,20},{20... | collective-permute-start | bytes 6291464 | tf_op jit(solution)/shard_map/ppermute | solution.py:15
  115.0 13.1 %all-to-all-start = ((f32[16,2,32]{2,1,0:T(2,128)}), f32[16,2,32]{2,1,0:T(2,128)S(1)}, u32[]{:S(2)}, u32[]{:S(2)}) async-start(f32[16,2,32]{2,1,0:T(2,128)} %copy.22), calls=%async_computation | async-start | bytes 32768 | tf_op jit(solution)/shard_map/all_to_all | solution.py:222
  128.9 4.4 %copy-start.1 = (bf16[4,256,3072]{2,1,0:T(8,128)(2,1)S(1)}, bf16[4,256,3072]{2,1,0:T(8,128)(2,1)}, u32[]{:S(2)}) copy-start(bf16[4,256,3072]{2,1,0:T(8,128)(2,1)} %copy-done) | copy-start | bytes 18874372

commit v4 on v3

--- a/solution.py
+++ b/solution.py
@@ -146,6 +146,44 @@
     )(own)
 
 
+def place_kernel(wide_ref, tokens_ref, scale_ref, routed_ref, scaled_ref):
+    rows = jnp.dot(wide_ref[0], tokens_ref[0], preferred_element_type=F32)
+    routed_ref[...] = rows.astype(BF)
+    scaled_ref[...] = (scale_ref[...] * rows).astype(BF)
+
+
+def place_rows(wide, tokens, scale, half):
+    groups, rows, toks = wide.shape
+    cut = half // 2
+    block = pl.BlockSpec((rows, cut), lambda g, j: (g, j))
+    return pl.pallas_call(
+        place_kernel,
+        grid=(groups, 2),
+        out_shape=[jax.ShapeDtypeStruct((groups * rows, half), BF)] * 2,
+        in_specs=[
+            pl.BlockSpec((1, rows, toks), lambda g, j: (g, 0, 0)),
+            pl.BlockSpec((1, toks, cut), lambda g, j: (g, 0, j)),
+            pl.BlockSpec((rows, 1), lambda g, j: (g, 0)),
+        ],
+        out_specs=[block, block],
+        compiler_params=pltpu.CompilerParams(vmem_limit_bytes=24 * 2**20),
+    )(wide, tokens, scale)
+
+
+def share_sum(x, axis, dim):
+    size, index = lax.axis_size(axis), lax.axis_index(axis)
+    bit = size // 2
+    while bit:
+        low, high = jnp.split(x, 2, axis=dim)
+        upper = lax.rem(index // bit, 2) == 1
+        sent = lax.ppermute(
+            jnp.where(upper, low, high), axis, [(i, i ^ bit) for i in range(size)]
+        )
+        x = jnp.where(upper, high, low) + sent
+        bit //= 2
+    return x
+
+
 def shards(out_grad, routes, route_weight, gate_pre, up_pre, down_weight):
     me = lax.axis_index("dp")
     expert = lax.axis_index("expert")
@@ -156,17 +194,13 @@
     half = width // 2
     first = me == 0
 
-    def ordered(mine, other):
-        return jnp.where(first, mine, other), jnp.where(first, other, mine)
-
     meta = jnp.concatenate([routes[0].astype(BF), route_weight[0]], axis=1)
     meta = jnp.pad(meta, ((0, 0), (0, 124)))
     low = jnp.concatenate([out_grad[0, :, :half], meta], axis=1)
     high = jnp.concatenate([out_grad[0, :, half:], meta], axis=1)
     keep = jnp.where(first, low, high)
     other = swap(jnp.where(first, high, low))
-    both = gather(jnp.stack(ordered(keep, other)))
-    tokens = both[..., :half]
+    both = gather(jnp.stack((keep, other)))
     meta = jnp.swapaxes(both[..., half : half + 4].astype(F32), 2, 3)
 
     hits = meta[:, :, :2] == expert.astype(F32)
@@ -183,13 +217,9 @@
     wide = place.reshape(2, n // group, group, cap, 1, tok) & eye[:, None, :, None]
     wide = wide.reshape(2 * n // group, group * cap, group * tok).astype(BF)
 
-    routed = lax.dot_general(
-        wide,
-        tokens.reshape(2 * n // group, group * tok, half),
-        (((2,), (1,)), ((0,), (0,))),
-        preferred_element_type=F32,
-    ).reshape(2 * rows, half)
-    routed = routed.astype(BF)
+    routed, scaled = place_rows(
+        wide, both.reshape(2 * n // group, group * tok, half + 128), scale, half
+    )
 
     gate = gate_pre[0, 0].astype(F32)
     upper = up_pre[0, 0].astype(F32)
@@ -197,30 +227,27 @@
     act = gate * sig
     slope = sig * (1.0 + gate * (1.0 - sig))
     hidden = (act * upper).astype(BF)
-    hidden_both = jnp.concatenate(ordered(hidden, swap(hidden)), axis=0)
+    hidden_both = jnp.concatenate((hidden, swap(hidden)), axis=0)
 
     back = lax.dot_general(
         routed, down_weight[0], (((1,), (1,)), ((), ())), preferred_element_type=F32
     ).reshape(2, rows, -1)
-    sent = lax.dynamic_index_in_dim(back, 1 - me, 0, keepdims=False).astype(BF)
-    back = lax.dynamic_index_in_dim(back, me, 0, keepdims=False) + swap(sent).astype(F32)
-
-    scaled = (scale * routed).astype(BF)
+    back = back[0] + swap(back[1].astype(BF)).astype(F32)
+
     down_grad = lax.dot_general(
         hidden_both, scaled, (((0,), (0,)), ((), ())), preferred_element_type=F32
     ).astype(BF)
 
-    my_scale = lax.dynamic_slice_in_dim(scale, me * rows, rows, 0)
+    my_scale = scale[:rows]
     hidden_grad = my_scale * back
     gate_grad = (hidden_grad * upper * slope).astype(BF)
     up_grad = (hidden_grad * act).astype(BF)
     score = jnp.sum(hidden.astype(F32) * back, axis=1).reshape(n, cap, 1)
-    my_place = lax.dynamic_index_in_dim(place, me, 0, keepdims=False)
-    my_hits = lax.dynamic_index_in_dim(hits, me, 0, keepdims=False)
-    tok_score = jnp.sum(jnp.where(my_place, score, 0.0), axis=1)
-    pair = jnp.where(my_hits, tok_score[:, None, :], 0.0)
-    pair = lax.all_to_all(pair, ("expert", "tensor"), split_axis=0, concat_axis=0, tiled=True)
-    route_grad = jnp.sum(pair, axis=0).T[None]
+    tok_score = jnp.sum(jnp.where(place[0], score, 0.0), axis=1)
+    pair = jnp.where(hits[0], tok_score[:, None, :], 0.0)
+    pair = pair.reshape(lax.axis_size("expert"), lax.axis_size("tensor"), 2, tok)
+    pair = share_sum(share_sum(pair, "tensor", 1), "expert", 0)
+    route_grad = pair.reshape(2, tok).T[None]
     return (route_grad, gate_grad[None, None], up_grad[None, None], down_grad[None])
 
 

time: 152 us -> 149 us (0.980)
  Pallas kernels: 59 us -> 63.5 us
  local copies, waits for them, and re-layouts: 15.5 us -> 11.8 us
  matrix products: 41.3 us -> 37.7 us
  other arithmetic: 17.3 us -> 14.3 us
  starting transfers between devices: 6.49 us -> 8.13 us
    ppermute x0 -> x4, waiting for transfers between devices: none -> 8.11 us  [share_sum(): lax.ppermute(jnp.where(upper, low, high), axis, [(i, i ^ bit) for i in ra...]
    ppermute x0 -> x4, starting transfers between devices: none -> 7.47 us  [share_sum(): lax.ppermute(jnp.where(upper, low, high), axis, [(i, i ^ bit) for i in ra...]
    all_to_all x1 -> x0, waiting for transfers between devices: 7.23 us -> none  [shards(): lax.all_to_all(pair, ('expert', 'tensor'), split_axis=0, concat_axis=0, t...]
    all_to_all x1 -> x0, starting transfers between devices: 5.83 us -> none  [shards(): lax.all_to_all(pair, ('expert', 'tensor'), split_axis=0, concat_axis=0, t...]
    dot_general x1 -> x0, matrix products: 4.59 us -> none  [shards(): lax.dot_general(wide, tokens.reshape(2 * n // group, group * tok, half),...]
    pallas_call x0 -> x1, Pallas kernels: none -> 4.55 us  [place_rows(): pl.pallas_call(place_kernel, grid=(groups, 2), out_shape=[jax.ShapeDtypeS...]
    select_n x2 -> x6, other arithmetic: 4.06 us -> 0.1 us  [the longest x1 0.05 us: shards(): keep = jnp.where(first, low, high)]
    slice x1 -> x4, local copies, waits for them, and re-layouts: 6.21 us -> 2.72 us  [the longest x1 1.63 us: shards(): back = back[0] + swap(back[1].astype(BF)).astype(F32)]
  transfers between devices with their start and end apart: 4 -> 7, of which waited for: 3 -> 6; matrix products, arithmetic and copies ran while one was open for 2% -> 1% of each run, Pallas kernels for 0% -> 0%
where the time goes in v4:
time: 149 us
  Pallas kernels  63.5 us (43%)
  matrix products  37.7 us (25%)
  other arithmetic  14.3 us (10%)
  waiting for transfers between devices  12.7 us (9%)
  local copies, waits for them, and re-layouts  11.8 us (8%)
  starting transfers between devices  8.13 us (5%)
    pallas_call x1, Pallas kernels, gather(): pl.pallas_call(functools.partial(gather_kernel, experts, depth), out_shap...  59 us
    dot_general x1, matrix products, shards(): lax.dot_general(hidden_both, scaled, (((0,), (0,)), ((), ())), preferred_...  19.7 us
    dot_general x1, matrix products, shards(): lax.dot_general(routed, down_weight[0], (((1,), (1,)), ((), ())), preferr...  18 us
    ppermute x4, waiting for transfers between devices, share_sum(): lax.ppermute(jnp.where(upper, low, high), axis, [(i, i ^ bit) for i in ra...  8.11 us
    reduce_sum x1, other arithmetic, shards(): score = jnp.sum(hidden.astype(F32) * back, axis=1).reshape(n, cap, 1)  8.02 us
    ppermute x4, starting transfers between devices, share_sum(): lax.ppermute(jnp.where(upper, low, high), axis, [(i, i ^ bit) for i in ra...  7.47 us
    unnamed x8, local copies, waits for them, and re-layouts  5.39 us
    ppermute x3, waiting for transfers between devices, swap(): return lax.ppermute(x, 'dp', [(0, 1), (1, 0)])  4.56 us
  transfers between devices with their start and end apart: 7, of which 6 were waited for; matrix products, arithmetic and copies ran while one was open for 1% of the time, Pallas kernels for 0%

profile of v4, /device:TPU:0, one launch (start us, length us, event | category | flops | bytes accessed | tf_op | source)
XLA Modules:
  0.0 148.9 jit_solution(4328570645273363910)
XLA Ops:
  0.6 0.7 convert_bitcast_fusion.2
  1.3 0.7 pad_maximum_fusion.5
  2.1 1.1 fusion.22
  4.8 0.8 pad_maximum_fusion.own_ref
  5.6 59.0 %shard_map.93 = bf16[2,16,32,3200]{3,2,1,0:T(8,128)(2,1)} custom-call(bf16[2,32,3200]{2,1,0:T(8,128)(2,1)} %pad_maximum_fusion.own_ref), custom_call_target="tpu_custom_call" | custom-call | tf_op jit(solution)/shard_map/pallas_call | solution.py:133
  64.6 1.0 convert_bitcast_fusion.1
  66.6 0.6 select_reduce_fusion.1
  68.7 1.6 %and.79 = pred[4,256,256]{2,1,0:T(8,128)(4,1)S(1)} reshape(pred[2,2,8,32,8,32]{5,4,3,2,1,0:T(8,128)(4,1)S(1)} %and.78) | data formatting | bytes 524288 | tf_op jit(solution)/shard_map/and | solution.py:217
  70.5 2.9 %copy-done = bf16[2,16,32,3200]{3,2,1,0:T(8,128)(2,1)S(1)} copy-done((bf16[2,16,32,3200]{3,2,1,0:T(8,128)(2,1)S(1)}, bf16[2,16,32,3200]{3,2,1,0:T(8,128)(2,1)}, u32[]{:S(2)}) %copy-start) | copy-done | bytes 6553624
  73.3 4.6 %shard_map.94 = (bf16[1024,3072]{1,0:T(8,128)(2,1)S(1)}, bf16[1024,3072]{1,0:T(8,128)(2,1)S(1)}) custom-call(bf16[4,256,256]{2,1,0:T(8,128)(2,1)S(1)} %and_convert_fusion.wide_ref, bf16[4,256,3200]{2,1,0:T(8,128)(2,1)S(1)} %bitcast.60, f32[1024,1]{1,0:T(8,128)S(1)} %reshape.124.scale_ref), custom_call_target="tpu_custom_call" | custom-call | tf_op jit(solution)/shard_map/pallas_call | solution.py:159
  77.9 18.0 %fusion = f32[1024,2048]{1,0:T(8,128)S(1)} fusion(bf16[1024,3072]{1,0:T(8,128)(2,1)S(1)} %get-tuple-element.6, bf16[1,2048,3072]{2,1,0:T(8,128)(2,1)} %param.11), kind=kOutput, calls=%fused_computation | convolution fusion | flops 12884901888 | bytes 27262976 | tf_op jit(solution)/shard_map/dot_general | solution.py:232
  95.9 1.6 %slice.69 = bf16[512,2048]{1,0:T(8,128)(2,1)} slice(f32[1024,2048]{1,0:T(8,128)S(1)} %fusion), slice={[512:1024], [0:2048]} | slice | bytes 4194304 | tf_op jit(solution)/shard_map/slice | solution.py:235
  97.5 2.5 %copy-done.2 = f32[1024,2048]{1,0:T(8,128)} copy-done((f32[1024,2048]{1,0:T(8,128)}, f32[1024,2048]{1,0:T(8,128)S(1)}, u32[]{:S(2)}) %copy-start.2) | copy-done | bytes 8388632
  100.5 4.1 %collective-permute-done.1 = bf16[512,2048]{1,0:T(8,128)(2,1)} collective-permute-done((bf16[512,2048]{1,0:T(8,128)(2,1)}, bf16[512,2048]{1,0:T(8,128)(2,1)}, u32[]{:S(2)}, u32[]{:S(2)}) %collective-permute-start.1) | collective-permute-done | bytes 2097184 | tf_op jit(solution)/shard_map/ppermute | solution.py:15
  104.6 8.0 %multiply_reduce_fusion = (f32[512]{0:T(512)S(1)}, bf16[512,2048]{1,0:T(8,128)(2,1)}, bf16[1,1,512,2048]{3,2,1,0:T(8,128)(2,1)}, bf16[1,1,512,2048]{3,2,1,0:T(8,128)(2,1)}) fusion(bf16[512,2048]{1,0:T(8,128)(2,1)} %collective-permute-done.1, f32[1024,2048]{1,0:T(8,128)} %copy-done.2, bf16[1,1,512,2048]{3,2,1,0:T(8,128)(2,1)S(1)} %copy-done.3, ...), kind=kLoop, calls=%fused_computation.22 | loop fusion | flops 24116736 | bytes 16781312 | tf_op jit(solution)/shard_map/reduce_sum | solution.py:245
  113.0 2.7 %collective-permute-start.2 = (f32[4,2,2,32]{3,2,1,0:T(2,128)S(1)}, f32[4,2,2,32]{3,2,1,0:T(2,128)S(1)}, u32[]{:S(2)}, u32[]{:S(2)}) collective-permute-start(f32[4,2,2,32]{3,2,1,0:T(2,128)S(1)} %broadcast_select_fusion.1), channel_id=1, source_target_pairs={{0,2},{1,3},{2,0},{3,1},{4,6},{5,7},{6,4},{7,5},{8,10},{9,11},{10,... | collective-permute-start | bytes 6152 | tf_op jit(solution)/shard_map/ppermute | solution.py:179
  115.7 1.9 %collective-permute-done.2 = f32[4,2,2,32]{3,2,1,0:T(2,128)S(1)} collective-permute-done((f32[4,2,2,32]{3,2,1,0:T(2,128)S(1)}, f32[4,2,2,32]{3,2,1,0:T(2,128)S(1)}, u32[]{:S(2)}, u32[]{:S(2)}) %collective-permute-start.2) | collective-permute-done | bytes 2080 | tf_op jit(solution)/shard_map/ppermute | solution.py:179
  117.6 1.7 %collective-permute-start.3 = (f32[4,1,2,32]{3,2,1,0:T(2,128)S(1)}, f32[4,1,2,32]{3,2,1,0:T(2,128)S(1)}, u32[]{:S(2)}, u32[]{:S(2)}) collective-permute-start(f32[4,1,2,32]{3,2,1,0:T(2,128)S(1)} %broadcast_select_fusion.2), channel_id=1, source_target_pairs={{0,1},{1,0},{2,3},{3,2},{4,5},{5,4},{6,7},{7,6},{8,9},{9,8},{10,11... | collective-permute-start | bytes 3080 | tf_op jit(solution)/shard_map/ppermute | solution.py:179
  119.3 2.0 %collective-permute-done.3 = f32[4,1,2,32]{3,2,1,0:T(2,128)S(1)} collective-permute-done((f32[4,1,2,32]{3,2,1,0:T(2,128)S(1)}, f32[4,1,2,32]{3,2,1,0:T(2,128)S(1)}, u32[]{:S(2)}, u32[]{:S(2)}) %collective-permute-start.3) | collective-permute-done | bytes 1056 | tf_op jit(solution)/shard_map/ppermute | solution.py:179
  121.3 1.5 %collective-permute-start.4 = (f32[2,1,2,32]{3,2,1,0:T(2,128)S(1)}, f32[2,1,2,32]{3,2,1,0:T(2,128)S(1)}, u32[]{:S(2)}, u32[]{:S(2)}) collective-permute-start(f32[2,1,2,32]{3,2,1,0:T(2,128)S(1)} %broadcast_select_fusion.3), channel_id=1, source_target_pairs={{0,8},{4,12},{8,0},{12,4},{1,9},{5,13},{9,1},{13,5},{2,10},{6,14},... | collective-permute-start | bytes 1544 | tf_op jit(solution)/shard_map/ppermute | solution.py:179
  122.8 2.1 %collective-permute-done.4 = f32[2,1,2,32]{3,2,1,0:T(2,128)S(1)} collective-permute-done((f32[2,1,2,32]{3,2,1,0:T(2,128)S(1)}, f32[2,1,2,32]{3,2,1,0:T(2,128)S(1)}, u32[]{:S(2)}, u32[]{:S(2)}) %collective-permute-start.4) | collective-permute-done | bytes 544 | tf_op jit(solution)/shard_map/ppermute | solution.py:179
  125.0 1.6 %collective-permute-start.5 = (f32[1,1,2,32]{3,2,1,0:T(2,128)S(1)}, f32[1,1,2,32]{3,2,1,0:T(2,128)S(1)}, u32[]{:S(2)}, u32[]{:S(2)}) collective-permute-start(f32[1,1,2,32]{3,2,1,0:T(2,128)S(1)} %broadcast_select_fusion.4), channel_id=1, source_target_pairs={{0,4},{4,0},{8,12},{12,8},{1,5},{5,1},{9,13},{13,9},{2,6},{6,2},{1... | collective-permute-start | bytes 776 | tf_op jit(solution)/shard_map/ppermute | solution.py:179
  126.5 2.1 %collective-permute-done.5 = f32[1,1,2,32]{3,2,1,0:T(2,128)S(1)} collective-permute-done((f32[1,1,2,32]{3,2,1,0:T(2,128)S(1)}, f32[1,1,2,32]{3,2,1,0:T(2,128)S(1)}, u32[]{:S(2)}, u32[]{:S(2)}) %collective-permute-start.5) | collective-permute-done | bytes 288 | tf_op jit(solution)/shard_map/ppermute | solution.py:179
  129.2 19.7 %convert_bitcast_fusion = bf16[1,2048,3072]{2,1,0:T(8,128)(2,1)} fusion(bf16[1024,3072]{1,0:T(8,128)(2,1)} %copy-done.1, bf16[512,2048]{1,0:T(8,128)(2,1)} %collective-permute-done.6, bf16[512,2048]{1,0:T(8,128)(2,1)} %get-tuple-element.9), kind=kOutput, calls=%fused_computation.2 | convolution fusion | flops 12899581952 | bytes 23068672 | tf_op jit(solution)/shard_map/dot_general | solution.py:237
  (42 shorter events, 5.7 us)
Async XLA Ops:
  3.2 1.6 %collective-permute-start = (bf16[32,3200]{1,0:T(8,128)(2,1)S(1)}, bf16[32,3200]{1,0:T(8,128)(2,1)S(1)}, u32[]{:S(2)}, u32[]{:S(2)}) collective-permute-start(bf16[32,3200]{1,0:T(8,128)(2,1)S(1)} %fusion.18), channel_id=1, source_target_pairs={{0,16},{16,0},{1,17},{17,1},{2,18},{18,2},{3,19},{19,3},{4,20},{20... | collective-permute-start | bytes 614408 | tf_op jit(solution)/shard_map/ppermute | solution.py:15
  70.4 2.9 %copy-start = (bf16[2,16,32,3200]{3,2,1,0:T(8,128)(2,1)S(1)}, bf16[2,16,32,3200]{3,2,1,0:T(8,128)(2,1)}, u32[]{:S(2)}) copy-start(bf16[2,16,32,3200]{3,2,1,0:T(8,128)(2,1)} %shard_map.93) | copy-start | bytes 19660804
  77.9 18.0 %copy-start.1 = (bf16[1024,3072]{1,0:T(8,128)(2,1)}, bf16[1024,3072]{1,0:T(8,128)(2,1)S(1)}, u32[]{:S(2)}) copy-start(bf16[1024,3072]{1,0:T(8,128)(2,1)S(1)} %get-tuple-element.7) | copy-start | bytes 18874372
  95.9 4.2 %copy-start.2 = (f32[1024,2048]{1,0:T(8,128)}, f32[1024,2048]{1,0:T(8,128)S(1)}, u32[]{:S(2)}) copy-start(f32[1024,2048]{1,0:T(8,128)S(1)} %fusion) | copy-start | bytes 25165828
  95.9 8.7 %copy-start.3 = (bf16[1,1,512,2048]{3,2,1,0:T(8,128)(2,1)S(1)}, bf16[1,1,512,2048]{3,2,1,0:T(8,128)(2,1)}, u32[]{:S(2)}) copy-start(bf16[1,1,512,2048]{3,2,1,0:T(8,128)(2,1)} %param.10) | copy-start | bytes 6291460
  100.1 4.5 %collective-permute-start.1 = (bf16[512,2048]{1,0:T(8,128)(2,1)}, bf16[512,2048]{1,0:T(8,128)(2,1)}, u32[]{:S(2)}, u32[]{:S(2)}) collective-permute-start(bf16[512,2048]{1,0:T(8,128)(2,1)} %slice.69), channel_id=1, source_target_pairs={{0,16},{16,0},{1,17},{17,1},{2,18},{18,2},{3,19},{19,3},{4,20},{20... | collective-permute-start | bytes 6291464 | tf_op jit(solution)/shard_map/ppermute | solution.py:15
  112.7 16.5 %collective-permute-start.6 = (bf16[512,2048]{1,0:T(8,128)(2,1)}, bf16[512,2048]{1,0:T(8,128)(2,1)}, u32[]{:S(2)}, u32[]{:S(2)}) collective-permute-start(bf16[512,2048]{1,0:T(8,128)(2,1)} %get-tuple-element.9), channel_id=1, source_target_pairs={{0,16},{16,0},{1,17},{17,1},{2,18},{18,2},{3,19},{19,3},{4,20},{20... | collective-permute-start | bytes 6291464 | tf_op jit(solution)/shard_map/ppermute | solution.py:15
  113.0 4.6 %collective-permute-start.2 = (f32[4,2,2,32]{3,2,1,0:T(2,128)S(1)}, f32[4,2,2,32]{3,2,1,0:T(2,128)S(1)}, u32[]{:S(2)}, u32[]{:S(2)}) collective-permute-start(f32[4,2,2,32]{3,2,1,0:T(2,128)S(1)} %broadcast_select_fusion.1), channel_id=1, source_target_pairs={{0,2},{1,3},{2,0},{3,1},{4,6},{5,7},{6,4},{7,5},{8,10},{9,11},{10,... | collective-permute-start | bytes 6152 | tf_op jit(solution)/shard_map/ppermute | solution.py:179
  117.6 3.7 %collective-permute-start.3 = (f32[4,1,2,32]{3,2,1,0:T(2,128)S(1)}, f32[4,1,2,32]{3,2,1,0:T(2,128)S(1)}, u32[]{:S(2)}, u32[]{:S(2)}) collective-permute-start(f32[4,1,2,32]{3,2,1,0:T(2,128)S(1)} %broadcast_select_fusion.2), channel_id=1, source_target_pairs={{0,1},{1,0},{2,3},{3,2},{4,5},{5,4},{6,7},{7,6},{8,9},{9,8},{10,11... | collective-permute-start | bytes 3080 | tf_op jit(solution)/shard_map/ppermute | solution.py:179
  121.3 3.6 %collective-permute-start.4 = (f32[2,1,2,32]{3,2,1,0:T(2,128)S(1)}, f32[2,1,2,32]{3,2,1,0:T(2,128)S(1)}, u32[]{:S(2)}, u32[]{:S(2)}) collective-permute-start(f32[2,1,2,32]{3,2,1,0:T(2,128)S(1)} %broadcast_select_fusion.3), channel_id=1, source_target_pairs={{0,8},{4,12},{8,0},{12,4},{1,9},{5,13},{9,1},{13,5},{2,10},{6,14},... | collective-permute-start | bytes 1544 | tf_op jit(solution)/shard_map/ppermute | solution.py:179
  125.0 3.6 %collective-permute-start.5 = (f32[1,1,2,32]{3,2,1,0:T(2,128)S(1)}, f32[1,1,2,32]{3,2,1,0:T(2,128)S(1)}, u32[]{:S(2)}, u32[]{:S(2)}) collective-permute-start(f32[1,1,2,32]{3,2,1,0:T(2,128)S(1)} %broadcast_select_fusion.4), channel_id=1, source_target_pairs={{0,4},{4,0},{8,12},{12,8},{1,5},{5,1},{9,13},{13,9},{2,6},{6,2},{1... | collective-permute-start | bytes 776 | tf_op jit(solution)/shard_map/ppermute | solution.py:179

commit v5 on v4

--- a/solution.py
+++ b/solution.py
@@ -170,20 +170,6 @@
     )(wide, tokens, scale)
 
 
-def share_sum(x, axis, dim):
-    size, index = lax.axis_size(axis), lax.axis_index(axis)
-    bit = size // 2
-    while bit:
-        low, high = jnp.split(x, 2, axis=dim)
-        upper = lax.rem(index // bit, 2) == 1
-        sent = lax.ppermute(
-            jnp.where(upper, low, high), axis, [(i, i ^ bit) for i in range(size)]
-        )
-        x = jnp.where(upper, high, low) + sent
-        bit //= 2
-    return x
-
-
 def shards(out_grad, routes, route_weight, gate_pre, up_pre, down_weight):
     me = lax.axis_index("dp")
     expert = lax.axis_index("expert")
@@ -245,9 +231,8 @@
     score = jnp.sum(hidden.astype(F32) * back, axis=1).reshape(n, cap, 1)
     tok_score = jnp.sum(jnp.where(place[0], score, 0.0), axis=1)
     pair = jnp.where(hits[0], tok_score[:, None, :], 0.0)
-    pair = pair.reshape(lax.axis_size("expert"), lax.axis_size("tensor"), 2, tok)
-    pair = share_sum(share_sum(pair, "tensor", 1), "expert", 0)
-    route_grad = pair.reshape(2, tok).T[None]
+    pair = lax.all_to_all(pair, ("expert", "tensor"), split_axis=0, concat_axis=0, tiled=True)
+    route_grad = jnp.sum(pair, axis=0).T[None]
     return (route_grad, gate_grad[None, None], up_grad[None, None], down_grad[None])
 
 

time: 149 us -> 147 us (0.987)
  blocking collectives: 0 us -> 13.1 us
  waiting for transfers between devices: 12.7 us -> 4.87 us
  starting transfers between devices: 8.13 us -> 0.66 us
    all_to_all x0 -> x1, blocking collectives: none -> 13.1 us  [shards(): lax.all_to_all(pair, ('expert', 'tensor'), split_axis=0, concat_axis=0, t...]
    ppermute x4 -> x0, waiting for transfers between devices: 8.11 us -> none  [share_sum(): lax.ppermute(jnp.where(upper, low, high), axis, [(i, i ^ bit) for i in ra...]
    ppermute x4 -> x0, starting transfers between devices: 7.47 us -> none  [share_sum(): lax.ppermute(jnp.where(upper, low, high), axis, [(i, i ^ bit) for i in ra...]
    unnamed x8 -> x9, local copies, waits for them, and re-layouts: 5.39 us -> 5.48 us
  transfers between devices with their start and end apart: 7 -> 3, of which waited for: 6 -> 2; matrix products, arithmetic and copies ran while one was open for 1% -> 1% of each run, Pallas kernels for 0% -> 0%
where the time goes in v5:
time: 147 us
  Pallas kernels  63.5 us (43%)
  matrix products  37.7 us (26%)
  other arithmetic  13.8 us (9%)
  blocking collectives  13.1 us (9%)
  local copies, waits for them, and re-layouts  12.5 us (9%)
  waiting for transfers between devices  4.87 us (3%)
    pallas_call x1, Pallas kernels, gather(): pl.pallas_call(functools.partial(gather_kernel, experts, depth), out_shap...  59 us
    dot_general x1, matrix products, shards(): lax.dot_general(hidden_both, scaled, (((0,), (0,)), ((), ())), preferred_...  19.7 us
    dot_general x1, matrix products, shards(): lax.dot_general(routed, down_weight[0], (((1,), (1,)), ((), ())), preferr...  18 us
    all_to_all x1, blocking collectives, shards(): lax.all_to_all(pair, ('expert', 'tensor'), split_axis=0, concat_axis=0, t...  13.1 us
    reduce_sum x1, other arithmetic, shards(): score = jnp.sum(hidden.astype(F32) * back, axis=1).reshape(n, cap, 1)  8.02 us
    unnamed x9, local copies, waits for them, and re-layouts  5.48 us
    ppermute x3, waiting for transfers between devices, swap(): return lax.ppermute(x, 'dp', [(0, 1), (1, 0)])  4.87 us
    pallas_call x1, Pallas kernels, place_rows(): pl.pallas_call(place_kernel, grid=(groups, 2), out_shape=[jax.ShapeDtypeS...  4.55 us
  transfers between devices with their start and end apart: 3, of which 2 were waited for; matrix products, arithmetic and copies ran while one was open for 1% of the time, Pallas kernels for 0%

profile of v5, /device:TPU:0, one launch (start us, length us, event | category | flops | bytes accessed | tf_op | source)
XLA Modules:
  0.0 146.9 jit_solution(5205902868854448209)
XLA Ops:
  0.6 0.7 convert_bitcast_fusion.2
  1.3 0.7 pad_maximum_fusion.5
  2.1 1.1 fusion.23
  3.2 0.5 collective-permute-start
  4.0 0.4 and.61
  4.4 0.5 collective-permute-done
  4.8 0.8 pad_maximum_fusion.own_ref
  5.6 59.0 %shard_map.93 = bf16[2,16,32,3200]{3,2,1,0:T(8,128)(2,1)} custom-call(bf16[2,32,3200]{2,1,0:T(8,128)(2,1)} %pad_maximum_fusion.own_ref), custom_call_target="tpu_custom_call" | custom-call | tf_op jit(solution)/shard_map/pallas_call | solution.py:133
  64.6 1.0 convert_bitcast_fusion.1
  66.0 0.6 reduce_or.9
  66.6 0.6 select_reduce_fusion.1
  67.5 0.5 reshape.116.scale_ref
  68.1 0.6 and.58
  68.7 1.6 %and.59 = pred[4,256,256]{2,1,0:T(8,128)(4,1)S(1)} reshape(pred[2,2,8,32,8,32]{5,4,3,2,1,0:T(8,128)(4,1)S(1)} %and.58) | data formatting | bytes 524288 | tf_op jit(solution)/shard_map/and | solution.py:203
  70.5 2.9 %copy-done = bf16[2,16,32,3200]{3,2,1,0:T(8,128)(2,1)S(1)} copy-done((bf16[2,16,32,3200]{3,2,1,0:T(8,128)(2,1)S(1)}, bf16[2,16,32,3200]{3,2,1,0:T(8,128)(2,1)}, u32[]{:S(2)}) %copy-start) | copy-done | bytes 6553624
  73.3 4.6 %shard_map.94 = (bf16[1024,3072]{1,0:T(8,128)(2,1)S(1)}, bf16[1024,3072]{1,0:T(8,128)(2,1)S(1)}) custom-call(bf16[4,256,256]{2,1,0:T(8,128)(2,1)S(1)} %and_convert_fusion.wide_ref, bf16[4,256,3200]{2,1,0:T(8,128)(2,1)S(1)} %bitcast.58, f32[1024,1]{1,0:T(8,128)S(1)} %reshape.116.scale_ref), custom_call_target="tpu_custom_call" | custom-call | tf_op jit(solution)/shard_map/pallas_call | solution.py:159
  77.9 18.0 %fusion = f32[1024,2048]{1,0:T(8,128)S(1)} fusion(bf16[1024,3072]{1,0:T(8,128)(2,1)S(1)} %get-tuple-element.6, bf16[1,2048,3072]{2,1,0:T(8,128)(2,1)} %param.11), kind=kOutput, calls=%fused_computation | convolution fusion | flops 12884901888 | bytes 27262976 | tf_op jit(solution)/shard_map/dot_general | solution.py:218
  95.9 1.6 %slice.72 = bf16[512,2048]{1,0:T(8,128)(2,1)} slice(f32[1024,2048]{1,0:T(8,128)S(1)} %fusion), slice={[512:1024], [0:2048]} | slice | bytes 4194304 | tf_op jit(solution)/shard_map/slice | solution.py:221
  97.5 2.5 %copy-done.2 = f32[1024,2048]{1,0:T(8,128)} copy-done((f32[1024,2048]{1,0:T(8,128)}, f32[1024,2048]{1,0:T(8,128)S(1)}, u32[]{:S(2)}) %copy-start.2) | copy-done | bytes 8388632
  100.1 4.4 %collective-permute-done.1 = bf16[512,2048]{1,0:T(8,128)(2,1)} collective-permute-done((bf16[512,2048]{1,0:T(8,128)(2,1)}, bf16[512,2048]{1,0:T(8,128)(2,1)}, u32[]{:S(2)}, u32[]{:S(2)}) %collective-permute-start.1) | collective-permute-done | bytes 2097184 | tf_op jit(solution)/shard_map/ppermute | solution.py:15
  104.6 8.0 %multiply_reduce_fusion = (f32[512]{0:T(512)S(1)}, bf16[512,2048]{1,0:T(8,128)(2,1)}, bf16[1,1,512,2048]{3,2,1,0:T(8,128)(2,1)}, bf16[1,1,512,2048]{3,2,1,0:T(8,128)(2,1)}) fusion(bf16[512,2048]{1,0:T(8,128)(2,1)} %collective-permute-done.1, f32[1024,2048]{1,0:T(8,128)} %copy-done.2, bf16[1,1,512,2048]{3,2,1,0:T(8,128)(2,1)S(1)} %copy-done.3, ...), kind=kLoop, calls=%fused_computation.22 | loop fusion | flops 24116736 | bytes 16781312 | tf_op jit(solution)/shard_map/reduce_sum | solution.py:231
  113.4 13.1 %all_to_all.5 = f32[16,2,32]{2,1,0:T(2,128)S(1)} all-to-all(f32[16,2,32]{2,1,0:T(2,128)S(1)} %copy.22), channel_id=1, replica_groups=mesh['dp'=2,'expert'=4,'tensor'=4] {'expert','tensor'}, dimensions={0} | all-to-all | bytes 8192 | tf_op jit(solution)/shard_map/all_to_all | solution.py:234
  126.6 0.6 copy.24
  127.2 19.7 %convert_bitcast_fusion = bf16[1,2048,3072]{2,1,0:T(8,128)(2,1)} fusion(bf16[1024,3072]{1,0:T(8,128)(2,1)} %copy-done.1, bf16[512,2048]{1,0:T(8,128)(2,1)} %collective-permute-done.2, bf16[512,2048]{1,0:T(8,128)(2,1)} %get-tuple-element.9), kind=kOutput, calls=%fused_computation.2 | convolution fusion | flops 12899581952 | bytes 23068672 | tf_op jit(solution)/shard_map/dot_general | solution.py:223
  (29 shorter events, 2.2 us)
Async XLA Ops:
  3.2 1.6 %collective-permute-start = (bf16[32,3200]{1,0:T(8,128)(2,1)S(1)}, bf16[32,3200]{1,0:T(8,128)(2,1)S(1)}, u32[]{:S(2)}, u32[]{:S(2)}) collective-permute-start(bf16[32,3200]{1,0:T(8,128)(2,1)S(1)} %fusion.19), channel_id=1, source_target_pairs={{0,16},{16,0},{1,17},{17,1},{2,18},{18,2},{3,19},{19,3},{4,20},{20... | collective-permute-start | bytes 614408 | tf_op jit(solution)/shard_map/ppermute | solution.py:15
  70.4 2.9 %copy-start = (bf16[2,16,32,3200]{3,2,1,0:T(8,128)(2,1)S(1)}, bf16[2,16,32,3200]{3,2,1,0:T(8,128)(2,1)}, u32[]{:S(2)}) copy-start(bf16[2,16,32,3200]{3,2,1,0:T(8,128)(2,1)} %shard_map.93) | copy-start | bytes 19660804
  77.9 18.0 %copy-start.1 = (bf16[1024,3072]{1,0:T(8,128)(2,1)}, bf16[1024,3072]{1,0:T(8,128)(2,1)S(1)}, u32[]{:S(2)}) copy-start(bf16[1024,3072]{1,0:T(8,128)(2,1)S(1)} %get-tuple-element.7) | copy-start | bytes 18874372
  95.9 4.2 %copy-start.2 = (f32[1024,2048]{1,0:T(8,128)}, f32[1024,2048]{1,0:T(8,128)S(1)}, u32[]{:S(2)}) copy-start(f32[1024,2048]{1,0:T(8,128)S(1)} %fusion) | copy-start | bytes 25165828
  95.9 8.7 %copy-start.3 = (bf16[1,1,512,2048]{3,2,1,0:T(8,128)(2,1)S(1)}, bf16[1,1,512,2048]{3,2,1,0:T(8,128)(2,1)}, u32[]{:S(2)}) copy-start(bf16[1,1,512,2048]{3,2,1,0:T(8,128)(2,1)} %param.10) | copy-start | bytes 6291460
  100.1 4.5 %collective-permute-start.1 = (bf16[512,2048]{1,0:T(8,128)(2,1)}, bf16[512,2048]{1,0:T(8,128)(2,1)}, u32[]{:S(2)}, u32[]{:S(2)}) collective-permute-start(bf16[512,2048]{1,0:T(8,128)(2,1)} %slice.72), channel_id=1, source_target_pairs={{0,16},{16,0},{1,17},{17,1},{2,18},{18,2},{3,19},{19,3},{4,20},{20... | collective-permute-start | bytes 6291464 | tf_op jit(solution)/shard_map/ppermute | solution.py:15
  112.6 14.7 %collective-permute-start.2 = (bf16[512,2048]{1,0:T(8,128)(2,1)}, bf16[512,2048]{1,0:T(8,128)(2,1)}, u32[]{:S(2)}, u32[]{:S(2)}) collective-permute-start(bf16[512,2048]{1,0:T(8,128)(2,1)} %get-tuple-element.9), channel_id=1, source_target_pairs={{0,16},{16,0},{1,17},{17,1},{2,18},{18,2},{3,19},{19,3},{4,20},{20... | collective-permute-start | bytes 6291464 | tf_op jit(solution)/shard_map/ppermute | solution.py:15
